TPU v7x, 32 devices: a whole 2x2x4 slice. The times are simulated.
32 devices in a mesh: tm: 8 (over y, x, core), rows: 4 (over z).
Axes of the slice: x: 2, y: 2, z: 4, core: 2. Of those that a mesh axis runs over, the one named last changes fastest.
Arguments:
- inputs: bfloat16 [8, 2048, 512], P('rows', 'tm'), may hold values from -6 to 6
- resets: int32 [8, 2048], P('rows', 'tm'), may hold values from 0 to 1, as said below
- norm_gains: float32 [2, 512], replicated, may hold values from 0.5 to 1.5
- lam_re: float32 [2, 384], replicated, may hold values from -0.5 to -0.0022097087
- lam_im: float32 [2, 384], replicated, may hold values from -3.140625 to 3.140625
- time_steps: float32 [2, 384], replicated, may hold values from 0.011048543 to 0.4
- b_re: bfloat16 [2, 512, 384], replicated, may hold values from -0.25 to 0.25
- b_im: bfloat16 [2, 512, 384], replicated, may hold values from -0.25 to 0.25
- c_re: bfloat16 [2, 384, 512], replicated, may hold values from -0.21875 to 0.21875
- c_im: bfloat16 [2, 384, 512], replicated, may hold values from -0.21875 to 0.21875
- skip_weight: float32 [2, 512], replicated, may hold values from -3 to 3
- glu_w: bfloat16 [2, 512, 512], replicated, may hold values from -0.25 to 0.25
- glu_bias: float32 [2, 512], replicated, may hold values from -3 to 3
- cotangent: bfloat16 [8, 2048, 512], P('rows', 'tm'), may hold values from -6 to 6
Outputs:
- output: bfloat16 [8, 2048, 512], P('rows', 'tm')
- input_grad: bfloat16 [8, 2048, 512], P('rows', 'tm')
- gain_grad: float32 [2, 512], replicated
- lam_re_grad: float32 [2, 384], replicated
- lam_im_grad: float32 [2, 384], replicated
- step_grad: float32 [2, 384], replicated
- b_re_grad: float32 [2, 512, 384], replicated
- b_im_grad: float32 [2, 512, 384], replicated
- c_re_grad: float32 [2, 384, 512], replicated
- c_im_grad: float32 [2, 384, 512], replicated
- skip_grad: float32 [2, 512], replicated
- glu_w_grad: float32 [2, 512, 512], replicated
- glu_bias_grad: float32 [2, 512], replicated
Inputs may be any that keep to these rules, and one draw needn't show every extreme that they name: `resets`: every row starts a document at its first position; in each aligned block of 2 rows, one row chosen by the seed has no other start.
All inputs are finite; a program needn't handle non-finite values.
Results may differ from a plain program's by a relative error of at most 0.012.
Values sent between devices are 32-bit elements; how exact they have to be, the bound alone decides.
A program may use at most 128 MiB of HBM per device.

v0:
```python
import jax
import jax.numpy as jnp
from jax import lax
from jax.sharding import PartitionSpec as P

NORM_EPS = 1e-05


def prefix(value, axis, combine, identity, reverse):
    count, position = (lax.axis_size(axis), lax.axis_index(axis))
    everything = jax.tree.map(lambda part: lax.all_gather(part, axis), value)
    start = jax.tree.map(
        lambda part, zero: jnp.broadcast_to(jnp.asarray(zero, part.dtype), part.shape),
        value,
        identity,
    )

    def step(k, before):
        at = count - 1 - k if reverse else k
        reached = at > position if reverse else at < position
        new = combine(before, jax.tree.map(lambda part: part[at], everything))
        return jax.tree.map(lambda a, b: jnp.where(reached, a, b), new, before)

    return lax.fori_loop(0, count, step, start)


def discretize(lam_re, lam_im, time_steps):
    growth = lam_re * time_steps
    angles = lam_im * time_steps
    magnitude = jnp.exp(growth)
    a_re = magnitude * jnp.cos(angles)
    a_im = magnitude * jnp.sin(angles)
    e_re = jnp.expm1(growth) * jnp.cos(angles) - 2.0 * jnp.sin(0.5 * angles) ** 2
    modulus = lam_re * lam_re + lam_im * lam_im
    q_re = (e_re * lam_re + a_im * lam_im) / modulus
    q_im = (a_im * lam_re - e_re * lam_im) / modulus
    return (a_re, a_im, q_re, q_im)


def combine(earlier, latter):
    dec_re = latter[0] * earlier[0] - latter[1] * earlier[1]
    dec_im = latter[0] * earlier[1] + latter[1] * earlier[0]
    sta_re = latter[0] * earlier[2] - latter[1] * earlier[3] + latter[2]
    sta_im = latter[0] * earlier[3] + latter[1] * earlier[2] + latter[3]
    return (dec_re, dec_im, sta_re, sta_im)


def normalize(hidden, gain_row):
    average = jnp.mean(hidden, axis=-1, keepdims=True)
    centred = hidden - average
    spread = jnp.mean(centred * centred, axis=-1, keepdims=True)
    return centred * lax.rsqrt(spread + NORM_EPS) * gain_row


def exact_gelu(values):
    return jax.nn.gelu(values, approximate=False)


def local_pass(v_re, v_im, dec_re, dec_im, kept_mask, forward):
    part_re = kept_mask[:, :, None] * dec_re
    part_im = kept_mask[:, :, None] * dec_im
    return lax.associative_scan(
        combine, (part_re, part_im, v_re, v_im), reverse=not forward, axis=1
    )


def settle(scanned, carry_re, carry_im):
    incoming_re = carry_re[:, None, :]
    incoming_im = carry_im[:, None, :]
    x_re = scanned[2] + scanned[0] * incoming_re - scanned[1] * incoming_im
    x_im = scanned[3] + scanned[0] * incoming_im + scanned[1] * incoming_re
    return (x_re, x_im)


def summarize(scanned, forward, first_keep):
    if forward:
        return tuple((member[:, -1] for member in scanned))
    return tuple((first_keep * member[:, 0] for member in scanned))


def carries(summary, section):
    unit_pair = (
        jnp.ones_like(summary[0]),
        jnp.zeros_like(summary[0]),
        jnp.zeros_like(summary[0]),
        jnp.zeros_like(summary[0]),
    )
    if section == 0:
        return prefix(
            (summary[0], summary[1], summary[2], summary[3]), "tm", combine, unit_pair, False
        )
    if section == 1:
        return prefix(
            (summary[0], summary[1], summary[2], summary[3]), "tm", combine, unit_pair, True
        )
    if section == 2:
        return prefix(
            (summary[0], summary[1], summary[2], summary[3]), "tm", combine, unit_pair, False
        )
    return prefix((summary[0], summary[1], summary[2], summary[3]), "tm", combine, unit_pair, True)


def prepare(hidden, weights):
    gain_row, lam_re, lam_im, time_steps, b_re, b_im, c_re, c_im, skip_row, glu_w, glu_bias = (
        weights
    )
    u_low = normalize(hidden, gain_row).astype(jnp.bfloat16)
    coeffs = discretize(lam_re, lam_im, time_steps)
    b_real = b_re.astype(jnp.float32)
    b_imag = b_im.astype(jnp.float32)
    input_matrix = jnp.concatenate(
        [coeffs[2] * b_real - coeffs[3] * b_imag, coeffs[2] * b_imag + coeffs[3] * b_real], axis=1
    ).astype(jnp.bfloat16)
    driven = jnp.einsum("rch,hk->rck", u_low, input_matrix, preferred_element_type=jnp.float32)
    state_count = lam_re.shape[0]
    return (u_low, coeffs, input_matrix, driven[..., :state_count], driven[..., state_count:])


def finish(hidden, u_low, x_re, x_im, weights):
    gain_row, lam_re, lam_im, time_steps, b_re, b_im, c_re, c_im, skip_row, glu_w, glu_bias = (
        weights
    )
    state_low = jnp.concatenate([x_re, x_im], axis=-1).astype(jnp.bfloat16)
    output_matrix = jnp.concatenate([c_re, -c_im], axis=0)
    pre_act = jnp.einsum(
        "rck,kh->rch", state_low, output_matrix, preferred_element_type=jnp.float32
    )
    pre_act = pre_act + skip_row * u_low.astype(jnp.float32)
    gelu_out = exact_gelu(pre_act)
    gelu_low = gelu_out.astype(jnp.bfloat16)
    pre_gate = (
        jnp.einsum("rch,hk->rck", gelu_low, glu_w, preferred_element_type=jnp.float32) + glu_bias
    )
    result = hidden + gelu_out * jax.nn.sigmoid(pre_gate)
    return (state_low, output_matrix, pre_act, gelu_out, gelu_low, pre_gate, result)


def layer_front(hidden, weights, mask_set, forward, section):
    u_low, coeffs, input_matrix, drive_re, drive_im = prepare(hidden, weights)
    kept_mask = mask_set[0] if forward else mask_set[1]
    scanned = local_pass(drive_re, drive_im, coeffs[0], coeffs[1], kept_mask, forward)
    incoming = carries(summarize(scanned, forward, mask_set[2]), section)
    x_re, x_im = settle(scanned, incoming[2], incoming[3])
    result = finish(hidden, u_low, x_re, x_im, weights)[-1]
    return (result, (incoming[2], incoming[3]))


def layer_back(d_out, hidden, weights, mask_set, forward, section, saved_pair):
    gain_row, lam_re, lam_im, time_steps, b_re, b_im, c_re, c_im, skip_row, glu_w, glu_bias = (
        weights
    )
    kept_f, kept_r, first_keep = mask_set
    u_low, coeffs, input_matrix, drive_re, drive_im = prepare(hidden, weights)
    a_re, a_im, q_re, q_im = coeffs
    scanned = local_pass(drive_re, drive_im, a_re, a_im, kept_f if forward else kept_r, forward)
    x_re, x_im = settle(scanned, saved_pair[0], saved_pair[1])
    state_low, output_matrix, pre_act, gelu_out, gelu_low, pre_gate, result = finish(
        hidden, u_low, x_re, x_im, weights
    )
    gate_open = jax.nn.sigmoid(pre_gate)
    ds_low = (d_out * gelu_out * gate_open * (1.0 - gate_open)).astype(jnp.bfloat16)
    bias_grad = jnp.sum(ds_low.astype(jnp.float32), axis=(0, 1))
    glu_grad = jnp.einsum("rch,rck->hk", gelu_low, ds_low, preferred_element_type=jnp.float32)
    d_gelu = d_out * gate_open + jnp.einsum(
        "rck,hk->rch", ds_low, glu_w, preferred_element_type=jnp.float32
    )
    _, gelu_pull = jax.vjp(exact_gelu, pre_act)
    dy_low = gelu_pull(d_gelu)[0].astype(jnp.bfloat16)
    skip_grad = jnp.sum(dy_low.astype(jnp.float32) * u_low.astype(jnp.float32), axis=(0, 1))
    out_grad = jnp.einsum("rck,rch->kh", state_low, dy_low, preferred_element_type=jnp.float32)
    state_count = a_re.shape[0]
    c_re_grad = out_grad[:state_count]
    c_im_grad = -out_grad[state_count:]
    d_state = jnp.einsum("rch,kh->rck", dy_low, output_matrix, preferred_element_type=jnp.float32)
    back_forward = not forward
    adj_scan = local_pass(
        d_state[..., :state_count],
        d_state[..., state_count:],
        a_re,
        -a_im,
        kept_f if back_forward else kept_r,
        back_forward,
    )
    adj_in = carries(summarize(adj_scan, back_forward, first_keep), 3 - section)
    mu_re, mu_im = settle(adj_scan, adj_in[2], adj_in[3])
    if forward:
        prev_re = kept_f[:, :, None] * jnp.concatenate(
            [saved_pair[0][:, None], x_re[:, :-1]], axis=1
        )
        prev_im = kept_f[:, :, None] * jnp.concatenate(
            [saved_pair[1][:, None], x_im[:, :-1]], axis=1
        )
    else:
        prev_re = kept_r[:, :, None] * jnp.concatenate(
            [x_re[:, 1:], saved_pair[0][:, None]], axis=1
        )
        prev_im = kept_r[:, :, None] * jnp.concatenate(
            [x_im[:, 1:], saved_pair[1][:, None]], axis=1
        )
    da_re = jnp.sum(prev_re * mu_re + prev_im * mu_im, axis=(0, 1))
    da_im = jnp.sum(prev_re * mu_im - prev_im * mu_re, axis=(0, 1))
    dv_low = jnp.concatenate([mu_re, mu_im], axis=-1).astype(jnp.bfloat16)
    matrix_grad = jnp.einsum("rch,rck->hk", u_low, dv_low, preferred_element_type=jnp.float32)
    grad_re = matrix_grad[:, :state_count]
    grad_im = matrix_grad[:, state_count:]
    b_real = b_re.astype(jnp.float32)
    b_imag = b_im.astype(jnp.float32)
    b_re_grad = q_re * grad_re + q_im * grad_im
    b_im_grad = q_re * grad_im - q_im * grad_re
    dq_re = jnp.sum(b_real * grad_re + b_imag * grad_im, axis=0)
    dq_im = jnp.sum(b_real * grad_im - b_imag * grad_re, axis=0)
    _, disc_pull = jax.vjp(discretize, lam_re, lam_im, time_steps)
    lam_re_grad, lam_im_grad, steps_grad = disc_pull((da_re, da_im, dq_re, dq_im))
    d_norm = dy_low.astype(jnp.float32) * skip_row
    d_norm = d_norm + jnp.einsum(
        "rck,hk->rch", dv_low, input_matrix, preferred_element_type=jnp.float32
    )
    _, norm_pull = jax.vjp(normalize, hidden, gain_row)
    d_hidden, gain_grad = norm_pull(d_norm)
    grads = (
        gain_grad,
        lam_re_grad,
        lam_im_grad,
        steps_grad,
        b_re_grad,
        b_im_grad,
        c_re_grad,
        c_im_grad,
        skip_grad,
        glu_grad,
        bias_grad,
    )
    return (d_out + d_hidden, grads)


def on_device(
    inputs,
    resets,
    norm_gains,
    lam_re,
    lam_im,
    time_steps,
    b_re,
    b_im,
    c_re,
    c_im,
    skip_weight,
    glu_w,
    glu_bias,
    cotangent,
):
    weights = (
        norm_gains,
        lam_re,
        lam_im,
        time_steps,
        b_re,
        b_im,
        c_re,
        c_im,
        skip_weight,
        glu_w,
        glu_bias,
    )
    layer_one = tuple((tensor[0] for tensor in weights))
    layer_two = tuple((tensor[1] for tensor in weights))
    kept_f = 1.0 - resets.astype(jnp.float32)
    kept_r = jnp.concatenate([kept_f[:, 1:], jnp.ones_like(kept_f[:, :1])], axis=1)
    mask_set = (kept_f, kept_r, kept_f[:, :1])
    first_in = inputs.astype(jnp.float32)
    middle, saved_one = layer_front(first_in, layer_one, mask_set, True, 0)
    final_out, saved_two = layer_front(middle, layer_two, mask_set, False, 1)
    d_middle, grads_two = layer_back(
        cotangent.astype(jnp.float32), middle, layer_two, mask_set, False, 1, saved_two
    )
    d_first, grads_one = layer_back(d_middle, first_in, layer_one, mask_set, True, 0, saved_one)
    stacked = tuple(
        (
            jnp.stack([first_item, second_item])
            for first_item, second_item in zip(grads_one, grads_two)
        )
    )
    totals = lax.psum(
        (
            stacked[0],
            stacked[1],
            stacked[2],
            stacked[3],
            stacked[4],
            stacked[5],
            stacked[6],
            stacked[7],
            stacked[8],
            stacked[9],
            stacked[10],
        ),
        ("tm", "rows"),
    )
    return (final_out.astype(jnp.bfloat16), d_first.astype(jnp.bfloat16)) + tuple(totals)


def solution(mesh):
    in_specs = (
        P("rows", "tm", None),
        P("rows", "tm"),
        P(),
        P(),
        P(),
        P(),
        P(),
        P(),
        P(),
        P(),
        P(),
        P(),
        P(),
        P("rows", "tm", None),
    )
    out_specs = (
        P("rows", "tm", None),
        P("rows", "tm", None),
        P(),
        P(),
        P(),
        P(),
        P(),
        P(),
        P(),
        P(),
        P(),
        P(),
        P(),
    )
    return jax.shard_map(
        on_device, mesh=mesh, in_specs=in_specs, out_specs=out_specs, check_vma=False
    )
```

profile of v0, /device:TPU:0, one launch (start us, length us, event | category | flops | bytes accessed | tf_op | source)
XLA Modules:
  0.0 1109.5 jit_solution(530295899219064268)
XLA Ops:
  66.6 2.8 add_add_fusion.9
  151.6 10.5 all-gather
  164.8 9.0 all-gather.1
  180.2 8.1 all-gather.2
  191.0 9.0 all-gather.3
  201.3 4.2 fusion.140
  239.5 3.9 slice.2603
  316.6 15.1 %pad.1004 = f32[2,128,384]{2,1,0:T(8,128)} pad(f32[2,64,384]{2,1,0:T(8,128)} %add.2402, f32[]{:T(128)} %constant.182.clone.1), padding=0_0_0x1_0_1x0_0_0 | pad | bytes 589828 | tf_op jit(solution)/shard_map/pad | solution.py:62
  345.0 2.8 pad.1035
  355.3 2.8 pad.1006
  368.0 6.9 rev.19
  374.9 6.9 rev.18
  381.8 3.9 rev.16
  385.7 4.0 rev.17
  389.7 8.1 all_gather.60
  397.8 9.0 all_gather.62
  406.8 8.1 all_gather.61
  414.8 9.0 all_gather.63
  425.4 3.1 fusion.136
  449.8 2.9 add_add_fusion.5
  547.5 2.8 pad.1069
  551.1 2.8 pad.1099
  559.3 8.1 all-gather.4
  570.1 9.0 all-gather.5
  582.2 2.8 pad.1070
  585.7 8.1 all-gather.6
  596.5 9.0 all-gather.7
  606.4 4.6 add_reduce_fusion
  615.8 4.4 convert_reduce_fusion.1
  620.3 3.3 convert_reduce_fusion.2
  623.6 3.1 add_convert_fusion.1
  638.6 4.0 slice.2939
  648.5 3.9 slice.2934
  658.3 2.8 add_add_fusion.3
  808.8 2.8 pad.1163
  811.6 2.9 pad.1164
  819.2 2.8 pad.1134
  835.2 5.1 rev.23
  840.3 6.8 rev.21
  847.2 6.8 rev.22
  854.0 6.8 rev.20
  860.8 8.1 all_gather.70
  868.9 9.0 all_gather.69
  877.9 8.1 all_gather.68
  885.9 9.0 all_gather.71
  915.9 42.3 %all-reduce.257 = (f32[2,512]{1,0:T(2,128)}, f32[2,384]{1,0:T(2,128)}, f32[2,384]{1,0:T(2,128)}, f32[2,384]{1,0:T(2,128)}, f32[2,512]{1,0:T(2,128)}, /*index=5*/f32[2,512]{1,0:T(2,128)}) all-reduce(f32[2,512]{1,0:T(2,128)S(1)} %pad_maximum_fusion.129, f32[2,384]{1,0:T(2,128)S(1)} %copy-done.384, ...), channel_id=1, replica_groups=mesh['tm'=8,'rows'=4] {'tm','rows'}, use_global_device_ids=true, to_apply=%region_18.19 | all-reduce | flops 5376 | bytes 43008 | tf_op jit(solution)/shard_map/psum | solution.py:283
  959.4 132.7 %all-reduce.261.cloned.1.call-done = (f32[2,512,384]{2,1,0:T(8,128)}, f32[2,512,384]{2,1,0:T(8,128)}, f32[2,384,512]{2,1,0:T(8,128)}, f32[2,384,512]{2,1,0:T(8,128)}, f32[2,512,512]{2,1,0:T(8,128)}) async-done(((f32[2,512,384]{2,1,0:T(8,128)}, f32[2,512,384]{2,1,0:T(8,128)}, f32[2,384,512]{2,1,0:T(8,128)}, f32[2,384,512]{2,1,0:T(8,128)}, f32[2,512,512]{2,1,0:T(8,128)}), (f32[2,512,384]{2,1,0:T(8,128)}, ...) | async-done | bytes 8388624 | tf_op jit(solution)/shard_map/psum | solution.py:283
  1092.2 2.8 copy.110
  (1987 shorter events, 644.6 us)
Async XLA Ops:
  7.2 10.1 copy-start.67
  7.2 1085.0 %all-reduce.261.cloned.1.call-start = ((), (), s32[]{:S(2)}) async-start(), calls=%async_computation | async-start | bytes 16777216 | tf_op jit(solution)/shard_map/psum | solution.py:283
  8.0 18.9 %copy-start.245 = (f32[2,256]{1,0:T(2,128)}, f32[2,256]{1,0:T(2,128)S(1)}, u32[]{:S(2)}) copy-start(f32[2,256]{1,0:T(2,128)S(1)} %convert_subtract_fusion.1) | copy-start | bytes 6148
  10.0 9.9 copy-start.247
  11.9 8.0 copy-start.279
  15.8 11.1 copy-start.271
  105.1 11.3 %copy-start.76 = (f32[2,63,384]{2,1,0:T(8,128)S(1)}, f32[2,63,384]{2,1,0:T(8,128)}, u32[]{:S(2)}) copy-start(f32[2,63,384]{2,1,0:T(8,128)} %slice.2442) | copy-start | bytes 580612
  145.4 16.8 %copy-start.137 = (f32[2,128,384]{2,1,0:T(8,128)S(1)}, f32[2,128,384]{2,1,0:T(8,128)}, u32[]{:S(2)}) copy-start(f32[2,128,384]{2,1,0:T(8,128)} %add.2325) | copy-start | bytes 1179652
  148.1 25.7 %copy-start.331 = (f32[2,1,384]{2,1,0:T(1,128)S(1)}, f32[2,1,384]{2,1,0:T(1,128)}, u32[]{:S(2)}) copy-start(f32[2,1,384]{2,1,0:T(1,128)} %get-tuple-element.1043) | copy-start | bytes 9220
  176.7 11.6 %copy-start.135 = (f32[2,128,384]{2,1,0:T(8,128)S(1)}, f32[2,128,384]{2,1,0:T(8,128)}, u32[]{:S(2)}) copy-start(f32[2,128,384]{2,1,0:T(8,128)} %add.2302) | copy-start | bytes 1179652
  205.5 9.2 copy-start.192
  219.6 391.4 %copy-start = (f32[2,256,512]{2,1,0:T(8,128)}, f32[2,256,512]{2,1,0:T(8,128)S(1)}, u32[]{:S(2)}) copy-start(f32[2,256,512]{2,1,0:T(8,128)S(1)} %get-tuple-element.956) | copy-start | bytes 3145732
  226.6 6.9 copy-start.110
  229.6 8.0 copy-start.119
  233.5 9.8 copy-start.121
  235.5 9.8 copy-start.118
  264.7 15.4 %copy-start.102 = (f32[2,127,384]{2,1,0:T(8,128)S(1)}, f32[2,127,384]{2,1,0:T(8,128)}, u32[]{:S(2)}) copy-start(f32[2,127,384]{2,1,0:T(8,128)} %slice.2597) | copy-start | bytes 1170436
  266.1 14.3 %copy-start.105 = (f32[2,127,384]{2,1,0:T(8,128)S(1)}, f32[2,127,384]{2,1,0:T(8,128)}, u32[]{:S(2)}) copy-start(f32[2,127,384]{2,1,0:T(8,128)} %slice.2718) | copy-start | bytes 1170436
  269.8 12.8 %copy-start.106 = (f32[2,127,384]{2,1,0:T(8,128)S(1)}, f32[2,127,384]{2,1,0:T(8,128)}, u32[]{:S(2)}) copy-start(f32[2,127,384]{2,1,0:T(8,128)} %slice.2760) | copy-start | bytes 1170436
  274.8 9.9 copy-start.108
  280.6 6.8 copy-start.360
  280.6 6.9 copy-start.358
  294.7 10.0 copy-start.75
  294.7 10.0 copy-start.77
  368.0 13.8 %copy-start.63 = (f32[2,256,384]{2,1,0:T(8,128)S(1)}, f32[2,256,384]{2,1,0:T(8,128)}, u32[]{:S(2)}) copy-start(f32[2,256,384]{2,1,0:T(8,128)} %add.2409) | copy-start | bytes 2359300
  374.9 10.8 copy-start.62
  385.7 39.6 %copy-start.66 = (f32[2,256,384]{2,1,0:T(8,128)S(1)}, f32[2,256,384]{2,1,0:T(8,128)}, u32[]{:S(2)}) copy-start(f32[2,256,384]{2,1,0:T(8,128)} %rev.19) | copy-start | bytes 2359300
  491.6 10.3 copy-start.154
  496.3 7.1 copy-start.398
  553.9 13.5 %copy-start.138 = (f32[2,128,384]{2,1,0:T(8,128)S(1)}, f32[2,128,384]{2,1,0:T(8,128)}, u32[]{:S(2)}) copy-start(f32[2,128,384]{2,1,0:T(8,128)} %add.2532) | copy-start | bytes 1179652
  555.8 23.4 %copy-start.334 = (f32[2,1,384]{2,1,0:T(1,128)S(1)}, f32[2,1,384]{2,1,0:T(1,128)}, u32[]{:S(2)}) copy-start(f32[2,1,384]{2,1,0:T(1,128)} %get-tuple-element.1025) | copy-start | bytes 9220
  579.2 14.6 %copy-start.136 = (f32[2,128,384]{2,1,0:T(8,128)S(1)}, f32[2,128,384]{2,1,0:T(8,128)}, u32[]{:S(2)}) copy-start(f32[2,128,384]{2,1,0:T(8,128)} %add.2509) | copy-start | bytes 1179652
  582.2 24.2 %copy-start.283 = (f32[2,256]{1,0:T(2,128)S(1)}, f32[2,256]{1,0:T(2,128)}, u32[]{:S(2)}) copy-start(f32[2,256]{1,0:T(2,128)} %copy-done.282) | copy-start | bytes 6148
  582.2 24.2 %copy-start.309 = (f32[2,1,384]{2,1,0:T(1,128)S(1)}, f32[2,1,384]{2,1,0:T(1,128)}, u32[]{:S(2)}) copy-start(f32[2,1,384]{2,1,0:T(1,128)} %broadcast_in_dim.22) | copy-start | bytes 9220
  582.2 24.2 %copy-start.310 = (f32[2,1,384]{2,1,0:T(1,128)S(1)}, f32[2,1,384]{2,1,0:T(1,128)}, u32[]{:S(2)}) copy-start(f32[2,1,384]{2,1,0:T(1,128)} %broadcast_in_dim.23) | copy-start | bytes 9220
  638.6 7.9 copy-start.100
  644.6 7.9 copy-start.120
  646.5 9.8 copy-start.122
  687.5 60.7 %copy-start.97 = (f32[2,127,384]{2,1,0:T(8,128)S(1)}, f32[2,127,384]{2,1,0:T(8,128)}, u32[]{:S(2)}) copy-start(f32[2,127,384]{2,1,0:T(8,128)} %slice.2923) | copy-start | bytes 1170436
  690.7 59.5 %copy-start.99 = (f32[2,127,384]{2,1,0:T(8,128)S(1)}, f32[2,127,384]{2,1,0:T(8,128)}, u32[]{:S(2)}) copy-start(f32[2,127,384]{2,1,0:T(8,128)} %slice.3044) | copy-start | bytes 1170436
  695.9 56.4 %copy-start.107 = (f32[2,127,384]{2,1,0:T(8,128)S(1)}, f32[2,127,384]{2,1,0:T(8,128)}, u32[]{:S(2)}) copy-start(f32[2,127,384]{2,1,0:T(8,128)} %slice.3085) | copy-start | bytes 1170436
  768.2 11.4 %copy-start.78 = (f32[2,63,384]{2,1,0:T(8,128)S(1)}, f32[2,63,384]{2,1,0:T(8,128)}, u32[]{:S(2)}) copy-start(f32[2,63,384]{2,1,0:T(8,128)} %slice.2942) | copy-start | bytes 580612
  808.8 7.5 copy-start.333
  847.2 47.8 %copy-start.228 = (f32[2,384]{1,0:T(2,128)S(1)}, f32[2,384]{1,0:T(2,128)}, u32[]{:S(2)}) copy-start(f32[2,384]{1,0:T(2,128)} %custom-call.7) | copy-start | bytes 9220
  847.2 47.8 %copy-start.229 = (f32[2,384]{1,0:T(2,128)S(1)}, f32[2,384]{1,0:T(2,128)}, u32[]{:S(2)}) copy-start(f32[2,384]{1,0:T(2,128)} %custom-call.6) | copy-start | bytes 9220
  915.0 43.1 %copy-start.3 = (f32[2,256,512]{2,1,0:T(8,128)S(1)}, f32[2,256,512]{2,1,0:T(8,128)}, u32[]{:S(2)}) copy-start(f32[2,256,512]{2,1,0:T(8,128)} %copy-done.2) | copy-start | bytes 3145732
  915.0 43.1 %copy-start.7 = (bf16[2,256,512]{2,1,0:T(8,128)(2,1)S(1)}, bf16[2,256,512]{2,1,0:T(8,128)(2,1)}, u32[]{:S(2)}) copy-start(bf16[2,256,512]{2,1,0:T(8,128)(2,1)} %param.35) | copy-start | bytes 1572868
  915.0 43.1 %copy-start.274 = (f32[2,256]{1,0:T(2,128)S(1)}, f32[2,256]{1,0:T(2,128)}, u32[]{:S(2)}) copy-start(f32[2,256]{1,0:T(2,128)} %copy-done.273) | copy-start | bytes 6148
  (374 other events, 1092.0 us)
Sparse Core Ops, SparseCore 0:
  910.5 181.5 all-reduce.260
where the time goes:
time: 1130 us; the launch traced here: 1110 us
  local copies, waits for them, and re-layouts  535 us (47%)
  other arithmetic  216 us (19%)
  blocking collectives  181 us (16%)
  waiting for transfers between devices  133 us (12%)
  matrix products  22.3 us (2%)
  between operations  21.3 us (2%)
    slice x448, local copies, waits for them, and re-layouts, local_pass(): lax.associative_scan(combine, (part_re, part_im, v_re, v_im), reverse=not...  280 us
    pad x224, local copies, waits for them, and re-layouts, local_pass(): lax.associative_scan(combine, (part_re, part_im, v_re, v_im), reverse=not...  167 us
    all_gather x16, blocking collectives, prefix(): everything = jax.tree.map(lambda part: lax.all_gather(part, axis), value)  139 us
    psum x1, waiting for transfers between devices, on_device(): lax.psum((stacked[0], stacked[1], stacked[2], stacked[3], stacked[4], sta...  133 us
    add x128, other arithmetic, local_pass(): lax.associative_scan(combine, (part_re, part_im, v_re, v_im), reverse=not...  75.2 us
    rev x8, local copies, waits for them, and re-layouts, local_pass(): lax.associative_scan(combine, (part_re, part_im, v_re, v_im), reverse=not...  47.2 us
    psum x1, blocking collectives, on_device(): lax.psum((stacked[0], stacked[1], stacked[2], stacked[3], stacked[4], sta...  42.3 us
    add x60, other arithmetic, combine(): sta_im = latter[0] * earlier[3] + latter[1] * earlier[2] + latter[3]  39.6 us
  transfers between devices with their start and end apart: 1, of which 1 were waited for; matrix products, arithmetic and copies ran while one was open for 1% of the time, Pallas kernels for 0%

commit v1 on v0

v1 whole, which is shorter than its diff:
```python
import functools
import math

import jax
import jax.numpy as jnp
from jax import lax
from jax.experimental import pallas as pl
from jax.experimental.pallas import tpu as pltpu
from jax.sharding import PartitionSpec as P

NORM_EPS = 1e-05
MESH = pl.DeviceIdType.MESH
F32 = jnp.float32
BF16 = jnp.bfloat16
SUB = 8
UNROLL = 4
TILE = 128
CLEAR = 99.0
STEPS = [128, 128, 256, 256, 128, 128]
ORDERS = [
    "zx", "xy", "yx", "zx", "zx", "xy", "zy", "yx", "yx", "zx", "xy", "xy", "xy", "yx", "xy",
    "zy", "xy", "xy", "zy", "xy", "xy", "yx", "yz",
]


class Refs:
    pass


def horner(value, coeffs):
    total = coeffs[-1]
    for coeff in coeffs[-2::-1]:
        total = total * value + coeff
    return total


def discretize(lam_re, lam_im, time_steps):
    growth = lam_re * time_steps
    angles = lam_im * time_steps
    square = angles * angles
    fact = math.factorial
    grow = growth * horner(growth, [1.0 / fact(k + 1) for k in range(8)])
    sine = angles * horner(square, [(-1.0) ** k / fact(2 * k + 1) for k in range(7)])
    dip = square * horner(square, [(-1.0) ** k / fact(2 * k + 2) for k in range(7)])
    cosine = 1.0 - dip
    magnitude = 1.0 + grow
    a_re = magnitude * cosine
    a_im = magnitude * sine
    e_re = grow * cosine - dip
    modulus = lam_re * lam_re + lam_im * lam_im
    q_re = (e_re * lam_re + a_im * lam_im) / modulus
    q_im = (a_im * lam_re - e_re * lam_im) / modulus
    return (a_re, a_im, q_re, q_im)


def cmul(a, b):
    return (a[0] * b[0] - a[1] * b[1], a[0] * b[1] + a[1] * b[0])


def dot(a, b):
    return jnp.dot(a, b, preferred_element_type=F32)


def dot_nt(a, b):
    return lax.dot_general(a, b, (((1,), (1,)), ((), ())), preferred_element_type=F32)


def dot_tn(a, b):
    return lax.dot_general(a, b, (((0,), (0,)), ((), ())), preferred_element_type=F32)


def fold(value):
    rows, cols = value.shape
    return jnp.sum(value.reshape(rows // SUB, SUB, cols), axis=0)


def gauss(y):
    size = jnp.abs(y) * (0.5**0.5)
    bell = jnp.exp(-0.5 * (y * y))
    t = 1.0 / (1.0 + 0.3275911 * size)
    tail = (0.5 * t * bell) * horner(
        t, [0.254829592, -0.284496736, 1.421413741, -1.453152027, 1.061405429]
    )
    cdf = jnp.where(y >= 0.0, 1.0 - tail, tail)
    return cdf, y * bell * ((2.0 * math.pi) ** -0.5)


class Chunk:
    def __init__(self, index, grad, rows, cols, bits):
        self.index, self.grad, self.rows, self.cols, self.bits = index, grad, rows, cols, bits
        self.width = cols[1] - cols[0]
        self.stages = []
        size, land = rows, 0
        for bit in bits:
            halved = size % (2 * SUB) == 0
            size = size // 2 if halved else size
            self.stages.append((bit, size, halved, land))
            land += size
        self.land_rows = land
        self.steps = [("sum", i) for i in range(len(bits))]
        self.steps += [("get", i) for i in reversed(range(len(bits))) if self.stages[i][2]]


def plan_chunks(n_tm, n_rows, width, P2):
    tm_bits, row_bits = int(math.log2(n_tm)), int(math.log2(n_rows))
    core = [("tm", 0)]
    half = (tm_bits - 1) // 2
    xs = [("tm", 1 + k) for k in range(half)]
    ys = [("tm", 1 + half + k) for k in range(tm_bits - 1 - half)]
    zs = [("rows", k) for k in range(row_bits)]
    axes = {"x": xs, "y": ys, "z": zs[:1]}

    def order(first, second):
        third = ({"x", "y", "z"} - {first, second}).pop()
        return core + axes[first] + axes[second] + axes[third] + zs[1:]

    chunks = {}
    count = 0
    plan, steps = iter(ORDERS), iter(STEPS)
    for l in (1, 0):
        for name, rows, cols in (("w", width, width), ("c", P2, width), ("b", width, P2)):
            step = next(steps)
            for k in range(0, cols, step):
                chunks[name, l, k] = Chunk(
                    count, (name, l), rows, (k, k + step), order(*next(plan))
                )
                count += 1
    chunks["s"] = Chunk(count, ("s", None), 2 * SUB, (0, width), order("y", "x"))
    return chunks


class Mover:
    RATE = {"c": 650e3, "x": 44e3, "y": 44e3, "z": 44e3, "mid": 44e3}
    DELAY = {"c": 0.9, "x": 2.3, "y": 2.3, "z": 2.3}
    AHEAD = 2.5

    def __init__(self, chunks, refs, lands, at, half_bits):
        self.chunks, self.refs, self.at, self.half_bits = chunks, refs, at, half_bits
        self.lands = lands
        self.now = 0.0
        self.free = {k: 0.0 for k in self.RATE}
        self.queue = {k: [] for k in self.DELAY}
        self.pending = []
        self.copies = {}
        self.sent = []
        self.starts = {}
        self.clear = None

    def coord(self, bit):
        return lax.rem(self.at[bit[0]] // (1 << bit[1]), 2)

    def peer(self, bit):
        own = self.at[bit[0]]
        return {bit[0]: own + (1 - 2 * self.coord(bit)) * (1 << bit[1])}

    def begin(self, chunk, level):
        key = (chunk.rows, tuple(chunk.bits[:level]))
        if key not in self.starts:
            if level == 0:
                self.starts[key] = 0
            else:
                bit, size, halved, _ = chunk.stages[level - 1]
                before = self.begin(chunk, level - 1)
                self.starts[key] = before + self.coord(bit) * size if halved else before
        return self.starts[key]

    def view(self, chunk, start, size, done=False):
        ref = self.refs[1 if done else 0][chunk.grad[0]]
        rows = pl.ds(pl.multiple_of(start, SUB) if not isinstance(start, int) else start, size)
        cols = pl.ds(chunk.cols[0], chunk.width)
        l = chunk.grad[1]
        return ref.at[rows, cols] if l is None else ref.at[l, rows, cols]

    def link(self, bit):
        if bit[0] == "rows":
            return "z"
        return "c" if bit[1] == 0 else ("x" if bit[1] <= self.half_bits else "y")

    def cost(self, chunk, k):
        bit, size, _, _ = chunk.stages[chunk.steps[k][1]]
        return size * chunk.width * 4 / self.RATE[self.link(bit)]

    def left(self, chunk, k):
        total = 0.0
        for j in range(k, len(chunk.steps)):
            bit = chunk.stages[chunk.steps[j][1]][0]
            total += self.cost(chunk, j) + self.DELAY[self.link(bit)]
        return total

    def push(self, chunk, k):
        bit = chunk.stages[chunk.steps[k][1]][0]
        self.queue[self.link(bit)].append((-self.left(chunk, k), chunk.index, k, chunk))

    def pump(self):
        for link, queue in self.queue.items():
            while queue and self.free[link] < self.now + self.AHEAD:
                item = min(queue, key=lambda entry: entry[:3])
                if self.clear is not None and link in ("x", "y"):
                    end = max(self.now, self.free[link]) + self.cost(item[3], item[2])
                    if end > self.clear:
                        break
                queue.remove(item)
                self.launch(item[3], item[2])

    def keep_clear(self, after):
        self.clear = None if after is None else self.now + after
        if after is None:
            self.pump()

    def launch(self, chunk, k):
        kind, i = chunk.steps[k]
        bit, size, halved, land = chunk.stages[i]
        if self.refs is not None:
            if kind == "sum":
                before = self.begin(chunk, i)
                if halved:
                    before = before + (1 - self.coord(bit)) * size
                src = self.view(chunk, before, size)
                dst = self.lands[chunk.index].at[pl.ds(land, size)]
            else:
                src = dst = self.view(chunk, self.begin(chunk, i + 1), size, True)
            copy = pltpu.make_async_remote_copy(
                src,
                dst,
                self.refs[2].at[chunk.index, k],
                self.refs[3].at[chunk.index, k],
                device_id=self.peer(bit),
                device_id_type=MESH,
            )
            copy.start()
            self.copies[chunk.index, k] = copy
        link = self.link(bit)
        cost = self.cost(chunk, k)
        far = link == "z" and bit[1] > 0
        began = max(self.now, self.free[link], self.free["mid"] if far else 0.0)
        self.free[link] = done = began + cost
        if far:
            self.free["mid"] = done = began + 2 * cost
        self.pending.append((done + self.DELAY[link], chunk.index, k, chunk))
        self.now += 0.04

    def finish(self, item):
        _, _, k, chunk = item
        kind, i = chunk.steps[k]
        bit, size, halved, land = chunk.stages[i]
        real = self.refs is not None
        copy = self.copies.get((chunk.index, k))
        if real:
            copy.wait_recv()
            if halved:
                self.sent.append(copy)
            else:
                copy.wait_send()
        self.now += 0.08
        more = k + 1 < len(chunk.steps)
        if kind == "get":
            if more:
                self.push(chunk, k + 1)
            self.pump()
            return
        start = self.begin(chunk, i + 1) if real else 0

        def add(off, rows):
            self.now += rows * chunk.width * 4 / 3e6
            if not real:
                return
            ref = self.view(chunk, start + off, rows)
            at = land + off
            at = pl.multiple_of(at, SUB) if not isinstance(at, int) else at
            last = i + 1 == len(chunk.bits)
            into = self.view(chunk, start + off, rows, True) if last else ref
            into[...] = ref[...] + self.lands[chunk.index][pl.ds(at, rows), :]

        if i + 1 < len(chunk.bits) and chunk.stages[i + 1][2]:
            half = size // 2
            mine = self.coord(chunk.stages[i + 1][0]) if real else 0
            add((1 - mine) * half, half)
            self.push(chunk, k + 1)
            self.pump()
            add(mine * half, half)
        else:
            add(0, size)
            if more:
                self.push(chunk, k + 1)
            self.pump()

    def first(self):
        return min(self.pending, key=lambda item: item[:3])

    def start(self, chunk):
        self.push(chunk, 0)
        self.pump()

    def run(self, spent):
        self.now += spent
        while self.pending and self.first()[0] <= self.now:
            item = self.first()
            self.pending.remove(item)
            self.finish(item)

    def drain(self):
        while self.pending:
            item = self.first()
            self.pending.remove(item)
            self.now = max(self.now, item[0])
            self.finish(item)
        if self.refs is not None:
            for copy in self.sent:
                copy.wait_send()


def kernel(cfg, *refs):
    tokens, width, states, rows_dev, group, n_tm, n_rows, chunks = cfg
    R = Refs()
    (
        R.inputs, R.resets_in, R.gains_in, R.lam_re_in, R.lam_im_in, R.steps_in, R.b_re, R.b_im,
        R.c_re, R.c_im, R.skip_in, R.glu_w, R.glu_b_in, R.cot, R.out, R.in_grad, R.small_o, R.b_o,
        R.c_o, R.w_o, R.xin, R.cin, R.wb_re, R.wb_im, R.wc, R.wg, R.h1, R.h2, R.z1, R.z2, R.r1,
        R.r2, R.u1, R.u2, R.v, R.x1, R.x2, R.s1, R.s2, R.gl1, R.gl2, R.gd1, R.gate1, R.prod1,
        R.d_mid, R.dy1, R.dy2, R.ds1, R.ds2, R.dv1, R.dv2, R.m1, R.m2, R.keep, R.stage, R.result, R.small_g,
        R.b_g, R.c_g, R.w_g, R.msg, R.got, R.in_sem, R.send_sem,
        R.recv_sem, R.put_sem, R.get_sem, R.resets, R.gains, R.lam_re, R.lam_im, R.steps, R.skip,
        R.glu_b,
        *lands,
    ) = refs
    segs = SUB
    per_seg = group // segs
    at = lax.axis_index("tm")
    P2 = 2 * states

    barrier = pltpu.get_barrier_semaphore()
    others = [lax.rem(at + k, n_tm) for k in range(1, n_tm)]
    for other in others:
        pl.semaphore_signal(barrier, inc=1, device_id={"tm": other}, device_id_type=MESH)
    row_at = lax.axis_index("rows")
    grads = {"b": R.b_g, "c": R.c_g, "w": R.w_g, "s": R.small_g}
    sums = {"b": R.b_o, "c": R.c_o, "w": R.w_o, "s": R.small_o}
    mover_refs = (grads, sums, R.put_sem, R.get_sem)
    half_bits = (int(math.log2(n_tm)) - 1) // 2
    mover = Mover(chunks, mover_refs, lands, {"tm": at, "rows": row_at}, half_bits)
    row_bits = int(math.log2(n_rows))
    for k in range(row_bits):
        pl.semaphore_signal(
            barrier, inc=1, device_id=mover.peer(("rows", k)), device_id_type=MESH
        )

    def load(k, src, dst):
        copy = pltpu.make_async_copy(src, dst, R.in_sem.at[k])
        copy.start()
        return copy

    cp_x = [load(r, R.inputs.at[r], R.xin.at[pl.ds(r * group, group)]) for r in range(rows_dev)]
    k0 = 2 * rows_dev + 5
    pairs = [
        (R.resets_in, R.resets), (R.lam_re_in, R.lam_re), (R.lam_im_in, R.lam_im),
        (R.steps_in, R.steps), (R.gains_in, R.gains), (R.skip_in, R.skip), (R.glu_b_in, R.glu_b),
    ]
    cp_small = [load(k0 + k, src, dst) for k, (src, dst) in enumerate(pairs)]
    k0 = rows_dev
    cp_b = [load(k0, R.b_re, R.wb_re), load(k0 + 1, R.b_im, R.wb_im)]
    cp_c = [
        load(k0 + 2, R.c_re, R.wc.at[:, pl.ds(0, states)]),
        load(k0 + 3, R.c_im, R.wc.at[:, pl.ds(states, states)]),
    ]
    cp_w = [load(k0 + 4, R.glu_w, R.wg)]
    cp_t = [
        load(k0 + 5 + r, R.cot.at[r], R.cin.at[pl.ds(r * group, group)])
        for r in range(rows_dev)
    ]

    for cp in cp_small:
        cp.wait()

    place_bits = int(math.log2(per_seg))
    i0 = lax.broadcasted_iota(jnp.int32, (group, group), 0)
    i1 = lax.broadcasted_iota(jnp.int32, (group, group), 1)
    hit = i1 == (i0 & (SUB - 1)) * per_seg + (i0 >> 3)
    gather = jnp.where(hit, 1.0, 0.0).astype(BF16)
    kept = 1.0 - R.resets[...].astype(F32)
    for r in range(rows_dev):
        spread = jnp.where(hit, jnp.broadcast_to(kept[r : r + 1], (group, group)), 0.0)
        R.keep[r * group : (r + 1) * group, :] = dot(
            spread.astype(BF16), jnp.ones((group, 128), BF16)
        )

    seg_id = lax.broadcasted_iota(jnp.int32, (SUB, 128), 0)

    def shift(value, forward, by=1):
        return pltpu.roll(value, by if forward else SUB - by, 0)

    def wide(mask, cols):
        return jnp.concatenate([mask] * (cols // 128), axis=1)

    def inside(forward, by):
        return seg_id >= by if forward else seg_id < SUB - by

    window, excl, total_mask = {}, {}, {}
    for r in range(rows_dev):
        places = [R.keep[r * group + j * SUB : r * group + (j + 1) * SUB] for j in range(per_seg)]
        while len(places) > 1:
            places = [a * b for a, b in zip(places[::2], places[1::2])]
        for forward in (True, False):
            run, seen = places[0], places[0]
            for by in (1, 2, 4):
                ok = inside(forward, by)
                window[r, forward, by] = jnp.where(ok, run, 0.0)
                seen = jnp.where(ok, seen * shift(seen, forward, by), seen)
                run = run * shift(run, forward, by)
            excl[r, forward] = jnp.where(inside(forward, 1), shift(seen, forward), 1.0)
            if forward:
                total_mask[r] = seen[SUB - 1 : SUB]

    L = []
    for l in range(2):
        lam = [n[l : l + 1, :] for n in (R.lam_re, R.lam_im, R.steps)]
        a_re, a_im, q_re, q_im = discretize(*lam)
        power = (a_re, a_im)
        for _ in range(place_bits):
            power = cmul(power, power)
        powers = {1: power}
        for by in (1, 2, 4):
            powers[2 * by] = cmul(powers[by], powers[by])
        for forward in (True, False):
            index = wide(seg_id if forward else SUB - 1 - seg_id, states)
            at_seg = (jnp.ones((SUB, states), F32), jnp.zeros((SUB, states), F32))
            for by in (1, 2, 4):
                more = cmul(at_seg, powers[by])
                at_seg = tuple(
                    jnp.where((index & by) != 0, m, o) for m, o in zip(more, at_seg)
                )
            powers[forward, 0] = at_seg
        L.append(dict(lam=lam, a=(a_re, a_im), q=(q_re, q_im), powers=powers, l=l))

    def input_matrix(layer, m_ref):
        q_re, q_im = layer["q"]
        l = layer["l"]
        step = 128
        for i in range(width // step):
            sl = slice(i * step, (i + 1) * step)
            br = R.wb_re[l, sl, :].astype(F32)
            bi = R.wb_im[l, sl, :].astype(F32)
            m_ref[sl, 0:states] = (q_re * br - q_im * bi).astype(BF16)
            m_ref[sl, states:P2] = (q_re * bi + q_im * br).astype(BF16)

    def scan_pass(r, layer, forward, start, sink):
        a = [jnp.broadcast_to(p, (SUB, states)) for p in layer["a"]]
        v_ref, keep_ref = R.v, R.keep

        def one(j, carry):
            base = pl.multiple_of(r * group + j * SUB, SUB)
            keep = wide(keep_ref[pl.ds(base, SUB), :], states)
            v = (v_ref[pl.ds(base, SUB), 0:states], v_ref[pl.ds(base, SUB), states:P2])
            if forward:
                held = (keep * carry[0], keep * carry[1])
                prod = cmul(a, held)
                x = (prod[0] + v[0], prod[1] + v[1])
                return x, held, x
            prod = cmul(a, carry)
            x = (prod[0] + v[0], prod[1] + v[1])
            held = (keep * x[0], keep * x[1])
            return x, carry, held

        pair = 2

        def body(i, carry):
            state, extra = carry
            if forward:
                js = [i * pair + k for k in range(pair)]
            else:
                js = [per_seg - 1 - (i * pair + k) for k in range(pair)]
            xs = []
            for j in js:
                x, held, state = one(j, state)
                xs.append(x)
                if sink is not None:
                    extra = sink.each(r * group + j * SUB, x, held, extra)
            if sink is not None:
                low = js[0] if forward else js[-1]
                ordered = xs if forward else xs[::-1]
                sink.pair(r * group + low * SUB, ordered)
            return state, extra

        extra0 = sink.zero() if sink is not None else ()
        return lax.fori_loop(0, per_seg // pair, body, (start, extra0), unroll=UNROLL)

    class Forward:
        def __init__(self, x_ref, s_ref):
            self.x_ref, self.s_ref = x_ref, s_ref

        def zero(self):
            return ()

        def each(self, base, x, held, extra):
            base = pl.multiple_of(base, SUB)
            self.x_ref[pl.ds(base, SUB), 0:states] = x[0]
            self.x_ref[pl.ds(base, SUB), states:P2] = x[1]
            return extra

        def pair(self, base, xs):
            base = pl.multiple_of(base, 2 * SUB)
            re = jnp.concatenate([x[0] for x in xs], axis=0)
            im = jnp.concatenate([x[1] for x in xs], axis=0)
            self.s_ref[pl.ds(base, 2 * SUB), 0:states] = re.astype(BF16)
            self.s_ref[pl.ds(base, 2 * SUB), states:P2] = (-im).astype(BF16)

    class Adjoint:
        def __init__(self, x_ref, d_ref):
            self.x_ref, self.d_ref = x_ref, d_ref

        def zero(self):
            return (jnp.zeros((SUB, states), F32), jnp.zeros((SUB, states), F32))

        def each(self, base, x, held, extra):
            base = pl.multiple_of(base, SUB)
            xv = (self.x_ref[pl.ds(base, SUB), 0:states], self.x_ref[pl.ds(base, SUB), states:P2])
            prod = cmul(xv, held)
            return (extra[0] + prod[0], extra[1] + prod[1])

        def pair(self, base, xs):
            base = pl.multiple_of(base, 2 * SUB)
            re = jnp.concatenate([x[0] for x in xs], axis=0)
            im = jnp.concatenate([x[1] for x in xs], axis=0)
            self.d_ref[pl.ds(base, 2 * SUB), 0:states] = re.astype(BF16)
            self.d_ref[pl.ds(base, 2 * SUB), states:P2] = (-im).astype(BF16)

    first_wait = [True]

    def send_carry(e, r, layer, forward, ends):
        seen = ends
        for by in (1, 2, 4):
            mask = wide(window[r, forward, by], states)
            prod = cmul(layer["powers"][by], tuple(shift(p, forward, by) for p in seen))
            seen = (seen[0] + mask * prod[0], seen[1] + mask * prod[1])
        ok = wide(inside(forward, 1), states)
        run = tuple(jnp.where(ok, shift(p, forward), 0.0) for p in seen)
        last = slice(SUB - 1, SUB) if forward else slice(0, 1)
        R.msg[e, r, :, 0:states] = seen[0][last]
        R.msg[e, r, :, states:P2] = seen[1][last]
        R.msg[e, r, :, P2 : P2 + 128] = total_mask[r]
        if first_wait[0]:
            pl.semaphore_wait(barrier, n_tm - 1 + row_bits)
            first_wait[0] = False
        copies = []
        for k, other in enumerate(others):
            copy = pltpu.make_async_remote_copy(
                R.msg.at[e, r],
                R.got.at[e, r, at],
                R.send_sem.at[e, r, k],
                R.recv_sem.at[e, r, k],
                device_id={"tm": other},
                device_id_type=MESH,
            )
            copy.start()
            copies.append(copy)
        return copies, run

    def take_carry(e, r, layer, forward, sent):
        copies, run = sent
        for copy in copies:
            copy.wait()
        span = layer["powers"][SUB]
        carry = (jnp.zeros((1, states), F32), jnp.zeros((1, states), F32))
        order = range(n_tm) if forward else range(n_tm - 1, -1, -1)
        for k in list(order)[:-1]:
            before = (at > k) if forward else (at < k)
            mask = wide(R.got[e, r, k, :, P2 : P2 + 128], states)
            prod = cmul(span, carry)
            new = (
                R.got[e, r, k, :, 0:states] + mask * prod[0],
                R.got[e, r, k, :, states:P2] + mask * prod[1],
            )
            carry = tuple(jnp.where(before, n, c) for n, c in zip(new, carry))
        prod = cmul(layer["powers"][forward, 0], carry)
        mask = wide(excl[r, forward], states)
        return (run[0] + mask * prod[0], run[1] + mask * prod[1])

    zero_state = (jnp.zeros((SUB, states), F32), jnp.zeros((SUB, states), F32))

    tiles = {
        r: [(slice(r * group + i, r * group + i + TILE), slice(i, i + TILE)) for i in range(0, group, TILE)]
        for r in range(rows_dev)
    }
    line = [slice(r * group, (r + 1) * group) for r in range(rows_dev)]
    rows = range(rows_dev)

    def norm_front(h, layer, z_ref, r_ref, u_ref, m_ref, sl):
        mean = jnp.mean(h, axis=1, keepdims=True)
        centred = h - mean
        var = jnp.mean(centred * centred, axis=1, keepdims=True)
        r = lax.rsqrt(var + NORM_EPS)
        z = centred * r
        u = (z * R.gains[layer["l"] : layer["l"] + 1, :]).astype(BF16)
        z_ref[sl, :] = z
        r_ref[sl, :] = jnp.broadcast_to(r, (r.shape[0], 128))
        u_ref[sl, :] = u
        R.v[sl, :] = dot(u, m_ref[...])

    def mixer(layer, s_ref, u_ref, gl_ref, sl):
        l = layer["l"]
        s = s_ref[sl, :]
        y = dot(s, R.wc[l]) + R.skip[l : l + 1, :] * u_ref[sl, :].astype(F32)
        cdf, dens = gauss(y)
        gelu = y * cdf
        low = gelu.astype(BF16)
        gl_ref[sl, :] = low
        pre = dot(low, R.wg[l]) + R.glu_b[l : l + 1, :]
        gate = 1.0 / (1.0 + jnp.exp(-pre))
        gated = gelu * gate
        return gated, cdf + dens, gate, gated * (1.0 - gate)

    def back_front(layer, d_out, slope, gate, prod, u_ref, ds_ref, dy_ref, sums, sl):
        l = layer["l"]
        ds = (d_out * prod).astype(BF16)
        ds_ref[sl, :] = ds
        d_gelu = d_out * gate + dot_nt(ds, R.wg[l])
        dy = (d_gelu * slope).astype(BF16)
        dy_ref[sl, :] = dy
        R.v[sl, :] = dot_nt(dy, R.wc[l])
        sums["bias"] = sums["bias"] + fold(ds.astype(F32))
        sums["skip"] = sums["skip"] + fold(dy.astype(F32) * u_ref[sl, :].astype(F32))

    def back_norm(layer, d_out, dv_ref, m_ref, dy_ref, z_ref, r_ref, sums, sl):
        l = layer["l"]
        dn = dy_ref[sl, :].astype(F32) * R.skip[l : l + 1, :] + dot_nt(dv_ref[sl, :], m_ref[...])
        z = z_ref[sl, :]
        sums["gain"] = sums["gain"] + fold(dn * z)
        w = dn * R.gains[l : l + 1, :]
        mean_w = jnp.mean(w, axis=1, keepdims=True)
        mean_wz = jnp.mean(w * z, axis=1, keepdims=True)
        r = wide(r_ref[sl, :], width)
        return d_out + r * (w - mean_w - z * mean_wz)

    def fresh():
        return {k: jnp.zeros((SUB, width), F32) for k in ("gain", "skip", "bias")}

    def start(name, l, first, count):
        for k in range(first, first + count, SUB):
            if (name, l, k) in chunks:
                mover.start(chunks[name, l, k])

    def product_grads(layer, gl_ref, ds_ref, s_ref, dy_ref):
        l = layer["l"]
        for name, left, right in (("w", gl_ref, ds_ref), ("c", s_ref, dy_ref)):
            for k in range(0, width, 256):
                grads[name][l, :, k : k + 256] = dot_tn(left[...], right[:, k : k + 256])
                start(name, l, k, 256)
                mover.run(0.25)

    def matrix_grads(layer, u_ref, dv_ref, da):
        l = layer["l"]
        q_re, q_im = layer["q"]
        full = dot_tn(u_ref[...], dv_ref[...])
        g_re, g_im = full[:, 0:states], full[:, states:P2]
        R.b_g[l, :, 0:states] = q_re * g_re + q_im * g_im
        R.b_g[l, :, states:P2] = q_re * g_im - q_im * g_re
        start("b", l, 0, P2)
        br, bi = R.wb_re[l].astype(F32), R.wb_im[l].astype(F32)
        dq_re = jnp.sum(fold(br * g_re + bi * g_im), axis=0, keepdims=True)
        dq_im = jnp.sum(fold(br * g_im - bi * g_re), axis=0, keepdims=True)
        da_re = jnp.sum(da[0], axis=0, keepdims=True)
        da_im = -jnp.sum(da[1], axis=0, keepdims=True)
        _, pull = jax.vjp(discretize, *layer["lam"])
        lam_grads = pull((da_re, da_im, dq_re, dq_im))
        for k, grad in enumerate(lam_grads):
            row = 6 + 2 * k + l
            R.small_g[row : row + 1, 0:states] = grad

    one, two = L
    for cp in cp_b:
        cp.wait()
    input_matrix(one, R.m1)
    for cp in cp_x:
        cp.wait()
    sent = {}
    for r in rows:
        for sl, part in tiles[r]:
            h = dot(gather[part, :], R.xin[line[r], :])
            R.h1[sl, :] = h
            norm_front(h, one, R.z1, R.r1, R.u1, R.m1, sl)
        ends, _ = scan_pass(r, one, True, zero_state, None)
        sent[0, r] = send_carry(0, r, one, True, ends)
    input_matrix(two, R.m2)
    for cp in cp_c + cp_w + cp_t:
        cp.wait()

    for r in rows:
        carry = take_carry(0, r, one, True, sent[0, r])
        scan_pass(r, one, True, carry, Forward(R.x1, R.s1))
        for sl, _ in tiles[r]:
            gated, slope, gate, prod = mixer(one, R.s1, R.u1, R.gl1, sl)
            R.gd1[sl, :] = slope
            R.gate1[sl, :] = gate
            R.prod1[sl, :] = prod
            h = R.h1[sl, :] + gated
            R.h2[sl, :] = h
            norm_front(h, two, R.z2, R.r2, R.u2, R.m2, sl)
        ends, _ = scan_pass(r, two, False, zero_state, None)
        sent[1, r] = send_carry(1, r, two, False, ends)

    sums2 = fresh()
    for r in rows:
        carry = take_carry(1, r, two, False, sent[1, r])
        scan_pass(r, two, False, carry, Forward(R.x2, R.s2))
        for sl, part in tiles[r]:
            gated, slope, gate, prod = mixer(two, R.s2, R.u2, R.gl2, sl)
            R.result[sl, :] = (R.h2[sl, :] + gated).astype(BF16)
            d_out = dot(gather[part, :], R.cin[line[r], :])
            R.d_mid[sl, :] = d_out
            back_front(two, d_out, slope, gate, prod, R.u2, R.ds2, R.dy2, sums2, sl)
        ends, _ = scan_pass(r, two, True, zero_state, None)
        sent[2, r] = send_carry(2, r, two, True, ends)
    product_grads(two, R.gl2, R.ds2, R.s2, R.dy2)

    sums1 = fresh()
    da2, da1 = Adjoint(R.x2, R.dv2).zero(), Adjoint(R.x1, R.dv1).zero()
    for r in rows:
        mover.run(0.5)
        carry = take_carry(2, r, two, True, sent[2, r])
        mover.run(0.5)
        _, da = scan_pass(r, two, True, carry, Adjoint(R.x2, R.dv2))
        da2 = (da2[0] + da[0], da2[1] + da[1])
        mover.run(0.3)
        for sl, _ in tiles[r]:
            d_mid = back_norm(two, R.d_mid[sl, :], R.dv2, R.m2, R.dy2, R.z2, R.r2, sums2, sl)
            R.d_mid[sl, :] = d_mid
            back_front(
                one, d_mid, R.gd1[sl, :], R.gate1[sl, :], R.prod1[sl, :],
                R.u1, R.ds1, R.dy1, sums1, sl,
            )
            mover.run(0.8)
        ends, _ = scan_pass(r, one, False, zero_state, None)
        mover.run(0.3)
        sent[3, r] = send_carry(3, r, one, False, ends)
    R.small_g[...] = jnp.zeros((2 * SUB, width), F32)
    matrix_grads(two, R.u2, R.dv2, da2)
    mover.run(1.0)
    product_grads(one, R.gl1, R.ds1, R.s1, R.dy1)

    for r in rows:
        mover.run(0.5)
        carry = take_carry(3, r, one, False, sent[3, r])
        mover.run(0.5)
        _, da = scan_pass(r, one, False, carry, Adjoint(R.x1, R.dv1))
        da1 = (da1[0] + da[0], da1[1] + da[1])
        mover.run(0.3)
        for sl, _ in tiles[r]:
            d_in = back_norm(one, R.d_mid[sl, :], R.dv1, R.m1, R.dy1, R.z1, R.r1, sums1, sl)
            R.stage[sl, :] = d_in.astype(BF16)
        mover.run(0.6)
    matrix_grads(one, R.u1, R.dv1, da1)
    for k, name in enumerate(("gain", "skip", "bias")):
        for l, sums in enumerate((sums1, sums2)):
            row = 2 * k + l
            R.small_g[row : row + 1, :] = jnp.sum(sums[name], axis=0, keepdims=True)
    mover.start(chunks["s"])
    mover.run(1.0)
    ungather = jnp.where(i1 == (i0 & (per_seg - 1)) * SUB + (i0 >> place_bits), 1.0, 0.0).astype(BF16)
    for r in rows:
        R.in_grad[r] = dot(ungather, R.stage[line[r], :]).astype(BF16)
    mover.run(0.5)
    for r in rows:
        R.out[r] = dot(ungather, R.result[line[r], :]).astype(BF16)
    mover.run(0.5)
    mover.drain()


def finish_kernel(states, out_v, in_grad_v, small_v, b_v, c_v, w_v, *refs):
    out, in_grad, gain, lam_re, lam_im, steps, b_re, b_im, c_re, c_im, skip, w, bias, sem = refs
    pairs = [
        (b_v.at[:, :, pl.ds(0, states)], b_re),
        (b_v.at[:, :, pl.ds(states, states)], b_im),
        (c_v.at[:, pl.ds(0, states)], c_re),
        (c_v.at[:, pl.ds(states, states)], c_im),
        (w_v, w),
        (out_v, out),
        (in_grad_v, in_grad),
    ]
    copies = [pltpu.make_async_copy(a, b, sem.at[k]) for k, (a, b) in enumerate(pairs)]
    for copy in copies:
        copy.start()
    for k, ref in enumerate((gain, skip, bias)):
        ref[...] = small_v[2 * k : 2 * k + 2, :]
    for k, ref in enumerate((lam_re, lam_im, steps)):
        ref[...] = small_v[6 + 2 * k : 8 + 2 * k, 0:states]
    for copy in copies:
        copy.wait()


def on_device(n_tm, n_rows, *args):
    inputs, lam_re = args[0], args[3]
    rows_dev, group, width = inputs.shape
    states = lam_re.shape[1]
    tokens = rows_dev * group
    P2 = 2 * states
    chunks = plan_chunks(n_tm, n_rows, width, P2)
    cfg = (tokens, width, states, rows_dev, group, n_tm, n_rows, chunks)
    vm = pl.BlockSpec(memory_space=pltpu.VMEM)
    hbm = pl.BlockSpec(memory_space=pl.ANY)
    far = pl.BlockSpec(memory_space=pltpu.HBM)
    in_specs = [far] * 14
    out_specs = [vm] * 6
    out_shape = [
        jax.ShapeDtypeStruct(inputs.shape, BF16),
        jax.ShapeDtypeStruct(inputs.shape, BF16),
        jax.ShapeDtypeStruct((2 * SUB, width), F32),
        jax.ShapeDtypeStruct((2, width, P2), F32),
        jax.ShapeDtypeStruct((2, P2, width), F32),
        jax.ShapeDtypeStruct((2, width, width), F32),
    ]

    def big(cols, dtype=F32):
        return pltpu.VMEM((tokens, cols), dtype)

    steps = max(len(chunk.steps) for chunk in chunks.values())
    scratch = [
        big(width, BF16), big(width, BF16),
        pltpu.VMEM((2, width, states), BF16), pltpu.VMEM((2, width, states), BF16),
        pltpu.VMEM((2, P2, width), BF16), pltpu.VMEM((2, width, width), BF16),
        big(width), big(width), big(width), big(width), big(128), big(128),
        big(width, BF16), big(width, BF16), big(P2), big(P2), big(P2),
        big(P2, BF16), big(P2, BF16), big(width, BF16), big(width, BF16),
        big(width), big(width), big(width), big(width),
        big(width, BF16), big(width, BF16), big(width, BF16), big(width, BF16),
        big(P2, BF16), big(P2, BF16),
        pltpu.VMEM((width, P2), BF16), pltpu.VMEM((width, P2), BF16),
        big(128), big(width, BF16), big(width, BF16),
        pltpu.VMEM((2 * SUB, width), F32), pltpu.VMEM((2, width, P2), F32),
        pltpu.VMEM((2, P2, width), F32), pltpu.VMEM((2, width, width), F32),
        pltpu.VMEM((4, rows_dev, 1, P2 + 128), F32),
        pltpu.VMEM((4, rows_dev, n_tm, 1, P2 + 128), F32),
        pltpu.SemaphoreType.DMA((2 * rows_dev + 12,)),
        pltpu.SemaphoreType.DMA((4, rows_dev, n_tm - 1)),
        pltpu.SemaphoreType.DMA((4, rows_dev, n_tm - 1)),
        pltpu.SemaphoreType.DMA((len(chunks), steps)), pltpu.SemaphoreType.DMA((len(chunks), steps)),
    ]
    for k in (1, 2, 3, 4, 5, 10, 12):
        scratch.append(pltpu.VMEM(args[k].shape, args[k].dtype))
    for chunk in chunks.values():
        scratch.append(pltpu.VMEM((chunk.land_rows, chunk.width), F32))
    held = pl.pallas_call(
        functools.partial(kernel, cfg),
        out_shape=[pltpu.VMEM(o.shape, o.dtype) for o in out_shape],
        in_specs=in_specs,
        out_specs=out_specs,
        scratch_shapes=scratch,
        compiler_params=pltpu.CompilerParams(
            collective_id=0, has_side_effects=True, vmem_limit_bytes=53 * 2**20
        ),
    )(*args)
    grads = [args[k] for k in range(2, 13)]
    final_shape = [out_shape[0]] * 2 + [jax.ShapeDtypeStruct(g.shape, F32) for g in grads]
    final_specs = [hbm, hbm] + [vm] * 4 + [hbm] * 4 + [vm, hbm, vm]
    return tuple(
        pl.pallas_call(
            functools.partial(finish_kernel, states),
            out_shape=final_shape,
            in_specs=[hbm, hbm, vm, hbm, hbm, hbm],
            out_specs=final_specs,
            scratch_shapes=[pltpu.SemaphoreType.DMA((7,))],
            compiler_params=pltpu.CompilerParams(vmem_limit_bytes=2**20),
        )(*held)
    )


def solution(mesh):
    rows = P("rows", "tm", None)
    in_specs = (rows, P("rows", "tm")) + (P(),) * 11 + (rows,)
    out_specs = (rows, rows) + (P(),) * 11
    return jax.shard_map(
        functools.partial(on_device, mesh.shape["tm"], mesh.shape["rows"]),
        mesh=mesh,
        in_specs=in_specs,
        out_specs=out_specs,
        check_vma=False,
    )
```

time: 1130 us -> 102 us (0.09); the launches traced: 1110 us -> 102 us
  local copies, waits for them, and re-layouts: 535 us -> 0 us
  other arithmetic: 216 us -> 0 us
  blocking collectives: 181 us -> 0 us
  waiting for transfers between devices: 133 us -> 0 us
  Pallas kernels: 0 us -> 101 us
  matrix products: 22.3 us -> 0 us
  between operations: 21.3 us -> 0.82 us
    slice x459 -> x0, local copies, waits for them, and re-layouts: 290 us -> none  [the longest x448 280 us: local_pass(): lax.associative_scan(combine, (part_re, part_im, v_re, v_im), reverse=not...]
    pad x224 -> x0, local copies, waits for them, and re-layouts: 167 us -> none  [local_pass(): lax.associative_scan(combine, (part_re, part_im, v_re, v_im), reverse=not...]
    all_gather x16 -> x0, blocking collectives: 139 us -> none  [prefix(): everything = jax.tree.map(lambda part: lax.all_gather(part, axis), value)]
    psum x1 -> x0, waiting for transfers between devices: 133 us -> none  [on_device(): lax.psum((stacked[0], stacked[1], stacked[2], stacked[3], stacked[4], sta...]
    add x214 -> x0, other arithmetic: 124 us -> none  [the longest x128 75.2 us: local_pass(): lax.associative_scan(combine, (part_re, part_im, v_re, v_im), reverse=not...]
    pallas_call x0 -> x2, Pallas kernels: none -> 101 us  [the longest x1 96.7 us: on_device(): pl.pallas_call(functools.partial(kernel, cfg), out_shape=[pltpu.VMEM(o.sh...]
    rev x8 -> x0, local copies, waits for them, and re-layouts: 47.2 us -> none  [local_pass(): lax.associative_scan(combine, (part_re, part_im, v_re, v_im), reverse=not...]
    psum x1 -> x0, blocking collectives: 42.3 us -> none  [on_device(): lax.psum((stacked[0], stacked[1], stacked[2], stacked[3], stacked[4], sta...]
  transfers between devices with their start and end apart: 1 -> 0, of which waited for: 1 -> 0; matrix products, arithmetic and copies ran while one was open for 1% -> 0% of each run, Pallas kernels for 0% -> 0%
where the time goes in v1:
time: 102 us
  Pallas kernels  101 us (99%)
    pallas_call x1, Pallas kernels, on_device(): pl.pallas_call(functools.partial(kernel, cfg), out_shape=[pltpu.VMEM(o.sh...  96.7 us
    pallas_call x1, Pallas kernels, on_device(): pl.pallas_call(functools.partial(finish_kernel, states), out_shape=final_...  4.29 us

profile of v1, /device:TPU:0, one launch (start us, length us, event | category | flops | bytes accessed | tf_op | source)
XLA Modules:
  0.0 101.9 jit_solution(418194272857313433)
XLA Ops:
  0.7 96.7 %shard_map.237 = (bf16[2,256,512]{2,1,0:T(8,128)(2,1)S(1)}, bf16[2,256,512]{2,1,0:T(8,128)(2,1)S(1)}, f32[16,512]{1,0:T(8,128)S(1)}, f32[2,512,768]{2,1,0:T(8,12...) custom-call(bf16[2,256,512]{2,1,0:T(8,128)(2,1)} %refs_0_.1, s32[2,256]{1,0:T(2,128)} %refs_1_.1, ...), custom_call_target="tpu_custom_call" | custom-call | tf_op jit(solution)/shard_map/pallas_call | solution.py:840
  97.4 4.3 %shard_map.238 = (bf16[2,256,512]{2,1,0:T(8,128)(2,1)}, bf16[2,256,512]{2,1,0:T(8,128)(2,1)}, f32[2,512]{1,0:T(2,128)}, f32[2,384]{1,0:T(2,128)}, f32[2,384]{1,0...) custom-call(bf16[2,256,512]{2,1,0:T(8,128)(2,1)S(1)} %get-tuple-elem, ...), custom_call_target="tpu_custom_call" | custom-call | tf_op jit(solution)/shard_map/pallas_call | solution.py:854

commit v2 on v1

--- a/solution.py
+++ b/solution.py
@@ -13,13 +13,13 @@
 F32 = jnp.float32
 BF16 = jnp.bfloat16
 SUB = 8
-UNROLL = 4
-TILE = 128
-CLEAR = 99.0
-STEPS = [128, 128, 256, 256, 128, 128]
+UNROLL = 16
+PUTS, GETS = 28, 18
+TILE = 256
+STEPS = [128, 128, 128, 128, 128, 128]
 ORDERS = [
-    "zx", "xy", "yx", "zx", "zx", "xy", "zy", "yx", "yx", "zx", "xy", "xy", "xy", "yx", "xy",
-    "zy", "xy", "xy", "zy", "xy", "xy", "yx", "yz",
+    "zy", "xy", "xy", "yx", "zy", "zx", "yx", "xy", "zy", "yx", "xy", "yz", "xy", "xz", "yx",
+    "xy", "xy", "xy", "zx", "zx", "yx", "xy", "yx", "xy", "yx", "xy", "yx", "xy",
 ]
 
 
@@ -77,7 +77,7 @@
 def gauss(y):
     size = jnp.abs(y) * (0.5**0.5)
     bell = jnp.exp(-0.5 * (y * y))
-    t = 1.0 / (1.0 + 0.3275911 * size)
+    t = pltpu.reciprocal(1.0 + 0.3275911 * size, approx=True)
     tail = (0.5 * t * bell) * horner(
         t, [0.254829592, -0.284496736, 1.421413741, -1.453152027, 1.061405429]
     )
@@ -130,8 +130,9 @@
 
 
 class Mover:
-    RATE = {"c": 650e3, "x": 44e3, "y": 44e3, "z": 44e3, "mid": 44e3}
-    DELAY = {"c": 0.9, "x": 2.3, "y": 2.3, "z": 2.3}
+    RATE = {"c": 650e3, "x": 46e3, "y": 46e3, "z": 46e3, "mid": 46e3}
+    DELAY = {"c": 0.8, "x": 1.7, "y": 1.7, "z": 1.7}
+    EXCHANGE = 3.2
     AHEAD = 2.5
 
     def __init__(self, chunks, refs, lands, at, half_bits):
@@ -142,9 +143,9 @@
         self.queue = {k: [] for k in self.DELAY}
         self.pending = []
         self.copies = {}
-        self.sent = []
         self.starts = {}
-        self.clear = None
+        self.clock = 0
+        self.gets, self.acked, self.puts, self.used = {}, {}, [], {}
 
     def coord(self, bit):
         return lax.rem(self.at[bit[0]] // (1 << bit[1]), 2)
@@ -191,25 +192,37 @@
         bit = chunk.stages[chunk.steps[k][1]][0]
         self.queue[self.link(bit)].append((-self.left(chunk, k), chunk.index, k, chunk))
 
+    def take_get(self, bit):
+        pool = self.gets.setdefault(bit, {})
+        for k, released in pool.items():
+            if released is not None and released < self.acked.get(bit, 0):
+                pool[k] = None
+                return k
+        k = sum(len(other) for other in self.gets.values())
+        pool[k] = None
+        return k
+
+    def take_put(self):
+        if True in self.puts:
+            k = self.puts.index(True)
+            self.puts[k] = False
+            return k
+        self.puts.append(False)
+        return len(self.puts) - 1
+
     def pump(self):
         for link, queue in self.queue.items():
             while queue and self.free[link] < self.now + self.AHEAD:
                 item = min(queue, key=lambda entry: entry[:3])
-                if self.clear is not None and link in ("x", "y"):
-                    end = max(self.now, self.free[link]) + self.cost(item[3], item[2])
-                    if end > self.clear:
-                        break
                 queue.remove(item)
                 self.launch(item[3], item[2])
-
-    def keep_clear(self, after):
-        self.clear = None if after is None else self.now + after
-        if after is None:
-            self.pump()
 
     def launch(self, chunk, k):
         kind, i = chunk.steps[k]
         bit, size, halved, land = chunk.stages[i]
+        put, get = self.take_put(), self.take_get(bit)
+        self.clock += 1
+        self.used[chunk.index, k] = (put, get, self.clock)
         if self.refs is not None:
             if kind == "sum":
                 before = self.begin(chunk, i)
@@ -222,8 +235,8 @@
             copy = pltpu.make_async_remote_copy(
                 src,
                 dst,
-                self.refs[2].at[chunk.index, k],
-                self.refs[3].at[chunk.index, k],
+                self.refs[2].at[put],
+                self.refs[3].at[get],
                 device_id=self.peer(bit),
                 device_id_type=MESH,
             )
@@ -242,15 +255,16 @@
     def finish(self, item):
         _, _, k, chunk = item
         kind, i = chunk.steps[k]
-        bit, size, halved, land = chunk.stages[i]
+        bit, size, _, land = chunk.stages[i]
         real = self.refs is not None
         copy = self.copies.get((chunk.index, k))
         if real:
-            copy.wait_recv()
-            if halved:
-                self.sent.append(copy)
-            else:
-                copy.wait_send()
+            copy.wait()
+        put, get, launched = self.used[chunk.index, k]
+        self.clock += 1
+        self.puts[put] = True
+        self.gets[bit][get] = self.clock
+        self.acked[bit] = max(self.acked.get(bit, 0), launched)
         self.now += 0.08
         more = k + 1 < len(chunk.steps)
         if kind == "get":
@@ -298,15 +312,23 @@
             self.pending.remove(item)
             self.finish(item)
 
+    def message(self):
+        return max(self.now, self.free["x"], self.free["y"]) + self.EXCHANGE
+
+    def until(self, time):
+        while self.pending and self.first()[0] <= time:
+            item = self.first()
+            self.pending.remove(item)
+            self.now = max(self.now, item[0])
+            self.finish(item)
+        self.now = max(self.now, time)
+
     def drain(self):
         while self.pending:
             item = self.first()
             self.pending.remove(item)
             self.now = max(self.now, item[0])
             self.finish(item)
-        if self.refs is not None:
-            for copy in self.sent:
-                copy.wait_send()
 
 
 def kernel(cfg, *refs):
@@ -357,12 +379,17 @@
     ]
     cp_small = [load(k0 + k, src, dst) for k, (src, dst) in enumerate(pairs)]
     k0 = rows_dev
-    cp_b = [load(k0, R.b_re, R.wb_re), load(k0 + 1, R.b_im, R.wb_im)]
+    cp_b = [load(k0, R.b_re.at[0], R.wb_re.at[0]), load(k0 + 1, R.b_im.at[0], R.wb_im.at[0])]
     cp_c = [
         load(k0 + 2, R.c_re, R.wc.at[:, pl.ds(0, states)]),
         load(k0 + 3, R.c_im, R.wc.at[:, pl.ds(states, states)]),
     ]
-    cp_w = [load(k0 + 4, R.glu_w, R.wg)]
+    k1 = 2 * rows_dev + 12
+    cp_w = [
+        load(k0 + 4, R.glu_w, R.wg),
+        load(k1, R.b_re.at[1], R.wb_re.at[1]),
+        load(k1 + 1, R.b_im.at[1], R.wb_im.at[1]),
+    ]
     cp_t = [
         load(k0 + 5 + r, R.cot.at[r], R.cin.at[pl.ds(r * group, group)])
         for r in range(rows_dev)
@@ -540,24 +567,24 @@
         if first_wait[0]:
             pl.semaphore_wait(barrier, n_tm - 1 + row_bits)
             first_wait[0] = False
-        copies = []
-        for k, other in enumerate(others):
+        for other in others:
             copy = pltpu.make_async_remote_copy(
                 R.msg.at[e, r],
                 R.got.at[e, r, at],
-                R.send_sem.at[e, r, k],
-                R.recv_sem.at[e, r, k],
+                R.send_sem.at[e, r],
+                R.recv_sem.at[e, r],
                 device_id={"tm": other},
                 device_id_type=MESH,
             )
             copy.start()
-            copies.append(copy)
-        return copies, run
+        return run, mover.message()
 
     def take_carry(e, r, layer, forward, sent):
-        copies, run = sent
-        for copy in copies:
-            copy.wait()
+        run, arrival = sent
+        mover.until(arrival)
+        slots = R.got.at[e, r, pl.ds(0, n_tm - 1)]
+        pltpu.make_async_copy(slots, slots, R.recv_sem.at[e, r]).wait()
+        pltpu.make_async_copy(slots, slots, R.send_sem.at[e, r]).wait()
         span = layer["powers"][SUB]
         carry = (jnp.zeros((1, states), F32), jnp.zeros((1, states), F32))
         order = range(n_tm) if forward else range(n_tm - 1, -1, -1)
@@ -604,7 +631,7 @@
         low = gelu.astype(BF16)
         gl_ref[sl, :] = low
         pre = dot(low, R.wg[l]) + R.glu_b[l : l + 1, :]
-        gate = 1.0 / (1.0 + jnp.exp(-pre))
+        gate = 0.5 * jnp.tanh(0.5 * pre) + 0.5
         gated = gelu * gate
         return gated, cdf + dens, gate, gated * (1.0 - gate)
 
@@ -644,7 +671,7 @@
             for k in range(0, width, 256):
                 grads[name][l, :, k : k + 256] = dot_tn(left[...], right[:, k : k + 256])
                 start(name, l, k, 256)
-                mover.run(0.25)
+                mover.run(0.15)
 
     def matrix_grads(layer, u_ref, dv_ref, da):
         l = layer["l"]
@@ -679,9 +706,9 @@
             norm_front(h, one, R.z1, R.r1, R.u1, R.m1, sl)
         ends, _ = scan_pass(r, one, True, zero_state, None)
         sent[0, r] = send_carry(0, r, one, True, ends)
-    input_matrix(two, R.m2)
     for cp in cp_c + cp_w + cp_t:
         cp.wait()
+    input_matrix(two, R.m2)
 
     for r in rows:
         carry = take_carry(0, r, one, True, sent[0, r])
@@ -707,6 +734,7 @@
             d_out = dot(gather[part, :], R.cin[line[r], :])
             R.d_mid[sl, :] = d_out
             back_front(two, d_out, slope, gate, prod, R.u2, R.ds2, R.dy2, sums2, sl)
+        mover.run(2.0)
         ends, _ = scan_pass(r, two, True, zero_state, None)
         sent[2, r] = send_carry(2, r, two, True, ends)
     product_grads(two, R.gl2, R.ds2, R.s2, R.dy2)
@@ -714,9 +742,8 @@
     sums1 = fresh()
     da2, da1 = Adjoint(R.x2, R.dv2).zero(), Adjoint(R.x1, R.dv1).zero()
     for r in rows:
-        mover.run(0.5)
         carry = take_carry(2, r, two, True, sent[2, r])
-        mover.run(0.5)
+        mover.run(0.3)
         _, da = scan_pass(r, two, True, carry, Adjoint(R.x2, R.dv2))
         da2 = (da2[0] + da[0], da2[1] + da[1])
         mover.run(0.3)
@@ -727,45 +754,45 @@
                 one, d_mid, R.gd1[sl, :], R.gate1[sl, :], R.prod1[sl, :],
                 R.u1, R.ds1, R.dy1, sums1, sl,
             )
-            mover.run(0.8)
+            mover.run(1.3)
         ends, _ = scan_pass(r, one, False, zero_state, None)
         mover.run(0.3)
         sent[3, r] = send_carry(3, r, one, False, ends)
     R.small_g[...] = jnp.zeros((2 * SUB, width), F32)
     matrix_grads(two, R.u2, R.dv2, da2)
-    mover.run(1.0)
+    mover.run(0.8)
     product_grads(one, R.gl1, R.ds1, R.s1, R.dy1)
 
     for r in rows:
-        mover.run(0.5)
         carry = take_carry(3, r, one, False, sent[3, r])
-        mover.run(0.5)
+        mover.run(0.3)
         _, da = scan_pass(r, one, False, carry, Adjoint(R.x1, R.dv1))
         da1 = (da1[0] + da[0], da1[1] + da[1])
         mover.run(0.3)
         for sl, _ in tiles[r]:
             d_in = back_norm(one, R.d_mid[sl, :], R.dv1, R.m1, R.dy1, R.z1, R.r1, sums1, sl)
             R.stage[sl, :] = d_in.astype(BF16)
-        mover.run(0.6)
+        mover.run(0.5)
     matrix_grads(one, R.u1, R.dv1, da1)
     for k, name in enumerate(("gain", "skip", "bias")):
         for l, sums in enumerate((sums1, sums2)):
             row = 2 * k + l
             R.small_g[row : row + 1, :] = jnp.sum(sums[name], axis=0, keepdims=True)
     mover.start(chunks["s"])
-    mover.run(1.0)
+    mover.run(0.8)
     ungather = jnp.where(i1 == (i0 & (per_seg - 1)) * SUB + (i0 >> place_bits), 1.0, 0.0).astype(BF16)
     for r in rows:
         R.in_grad[r] = dot(ungather, R.stage[line[r], :]).astype(BF16)
-    mover.run(0.5)
+    mover.run(0.3)
     for r in rows:
         R.out[r] = dot(ungather, R.result[line[r], :]).astype(BF16)
-    mover.run(0.5)
+    mover.run(0.3)
     mover.drain()
 
 
 def finish_kernel(states, out_v, in_grad_v, small_v, b_v, c_v, w_v, *refs):
-    out, in_grad, gain, lam_re, lam_im, steps, b_re, b_im, c_re, c_im, skip, w, bias, sem = refs
+    out, in_grad, gain, lam_re, lam_im, steps, b_re, b_im, c_re, c_im, skip, w, bias = refs[:13]
+    sem, *held = refs[13:]
     pairs = [
         (b_v.at[:, :, pl.ds(0, states)], b_re),
         (b_v.at[:, :, pl.ds(states, states)], b_im),
@@ -778,10 +805,11 @@
     copies = [pltpu.make_async_copy(a, b, sem.at[k]) for k, (a, b) in enumerate(pairs)]
     for copy in copies:
         copy.start()
-    for k, ref in enumerate((gain, skip, bias)):
-        ref[...] = small_v[2 * k : 2 * k + 2, :]
-    for k, ref in enumerate((lam_re, lam_im, steps)):
-        ref[...] = small_v[6 + 2 * k : 8 + 2 * k, 0:states]
+    for k, (ref, target) in enumerate(zip(held, (gain, skip, bias, lam_re, lam_im, steps))):
+        ref[...] = small_v[2 * k : 2 * k + 2, 0 : ref.shape[1]]
+        copy = pltpu.make_async_copy(ref, target, sem.at[len(pairs) + k])
+        copy.start()
+        copies.append(copy)
     for copy in copies:
         copy.wait()
 
@@ -811,7 +839,7 @@
     def big(cols, dtype=F32):
         return pltpu.VMEM((tokens, cols), dtype)
 
-    steps = max(len(chunk.steps) for chunk in chunks.values())
+    bits = int(math.log2(n_tm * n_rows))
     scratch = [
         big(width, BF16), big(width, BF16),
         pltpu.VMEM((2, width, states), BF16), pltpu.VMEM((2, width, states), BF16),
@@ -828,10 +856,9 @@
         pltpu.VMEM((2, P2, width), F32), pltpu.VMEM((2, width, width), F32),
         pltpu.VMEM((4, rows_dev, 1, P2 + 128), F32),
         pltpu.VMEM((4, rows_dev, n_tm, 1, P2 + 128), F32),
-        pltpu.SemaphoreType.DMA((2 * rows_dev + 12,)),
-        pltpu.SemaphoreType.DMA((4, rows_dev, n_tm - 1)),
-        pltpu.SemaphoreType.DMA((4, rows_dev, n_tm - 1)),
-        pltpu.SemaphoreType.DMA((len(chunks), steps)), pltpu.SemaphoreType.DMA((len(chunks), steps)),
+        pltpu.SemaphoreType.DMA((2 * rows_dev + 14,)),
+        pltpu.SemaphoreType.DMA((4, rows_dev)), pltpu.SemaphoreType.DMA((4, rows_dev)),
+        pltpu.SemaphoreType.DMA((PUTS,)), pltpu.SemaphoreType.DMA((bits * GETS,)),
     ]
     for k in (1, 2, 3, 4, 5, 10, 12):
         scratch.append(pltpu.VMEM(args[k].shape, args[k].dtype))
@@ -849,14 +876,16 @@
     )(*args)
     grads = [args[k] for k in range(2, 13)]
     final_shape = [out_shape[0]] * 2 + [jax.ShapeDtypeStruct(g.shape, F32) for g in grads]
-    final_specs = [hbm, hbm] + [vm] * 4 + [hbm] * 4 + [vm, hbm, vm]
+    final_specs = [hbm] * 13
     return tuple(
         pl.pallas_call(
             functools.partial(finish_kernel, states),
             out_shape=final_shape,
             in_specs=[hbm, hbm, vm, hbm, hbm, hbm],
             out_specs=final_specs,
-            scratch_shapes=[pltpu.SemaphoreType.DMA((7,))],
+            scratch_shapes=[pltpu.SemaphoreType.DMA((13,))]
+            + [pltpu.VMEM((2, width), F32)] * 3
+            + [pltpu.VMEM((2, states), F32)] * 3,
             compiler_params=pltpu.CompilerParams(vmem_limit_bytes=2**20),
         )(*held)
     )

time: 102 us -> 93.2 us (0.914)
  Pallas kernels: 101 us -> 92.2 us
    pallas_call x1, Pallas kernels: 96.7 us -> 88.5 us  [on_device(): pl.pallas_call(functools.partial(kernel, cfg), out_shape=[pltpu.VMEM(o.sh...]
where the time goes in v2:
time: 93.2 us; the launch traced here: 93 us
  Pallas kernels  92.2 us (99%)
    pallas_call x1, Pallas kernels, on_device(): pl.pallas_call(functools.partial(kernel, cfg), out_shape=[pltpu.VMEM(o.sh...  88.5 us
    pallas_call x1, Pallas kernels, on_device(): pl.pallas_call(functools.partial(finish_kernel, states), out_shape=final_...  3.74 us

profile of v2, /device:TPU:0, one launch (start us, length us, event | category | flops | bytes accessed | tf_op | source)
XLA Modules:
  0.0 93.0 jit_solution(16981423160489921115)
XLA Ops:
  0.7 88.5 %shard_map.237 = (bf16[2,256,512]{2,1,0:T(8,128)(2,1)S(1)}, bf16[2,256,512]{2,1,0:T(8,128)(2,1)S(1)}, f32[16,512]{1,0:T(8,128)S(1)}, f32[2,512,768]{2,1,0:T(8,12...) custom-call(bf16[2,256,512]{2,1,0:T(8,128)(2,1)} %refs_0_.1, s32[2,256]{1,0:T(2,128)} %refs_1_.1, ...), custom_call_target="tpu_custom_call" | custom-call | tf_op jit(solution)/shard_map/pallas_call | solution.py:867
  89.1 3.7 %shard_map.238 = (bf16[2,256,512]{2,1,0:T(8,128)(2,1)}, bf16[2,256,512]{2,1,0:T(8,128)(2,1)}, f32[2,512]{1,0:T(2,128)}, f32[2,384]{1,0:T(2,128)}, f32[2,384]{1,0...) custom-call(bf16[2,256,512]{2,1,0:T(8,128)(2,1)S(1)} %get-tuple-elem, ...), custom_call_target="tpu_custom_call" | custom-call | tf_op jit(solution)/shard_map/pallas_call | solution.py:881

commit v3 on v2

--- a/solution.py
+++ b/solution.py
@@ -14,12 +14,12 @@
 BF16 = jnp.bfloat16
 SUB = 8
 UNROLL = 16
-PUTS, GETS = 28, 18
+PUTS, GETS = 24, 15
 TILE = 256
-STEPS = [128, 128, 128, 128, 128, 128]
+STEPS = [256, 128, 128, 256, 128, 128]
 ORDERS = [
-    "zy", "xy", "xy", "yx", "zy", "zx", "yx", "xy", "zy", "yx", "xy", "yz", "xy", "xz", "yx",
-    "xy", "xy", "xy", "zx", "zx", "yx", "xy", "yx", "xy", "yx", "xy", "yx", "xy",
+    "zy", "XY", "yx", "xy", "YX", "ZX", "ZY", "yx", "yx", "yx", "YX", "XY", "XY", "yx", "xz",
+    "xy", "YX", "zx", "YX", "YX", "yx", "xy", "xy", "xz",
 ]
 
 
@@ -86,17 +86,20 @@
 
 
 class Chunk:
-    def __init__(self, index, grad, rows, cols, bits):
-        self.index, self.grad, self.rows, self.cols, self.bits = index, grad, rows, cols, bits
+    def __init__(self, index, grad, rows, cols, groups):
+        self.index, self.grad, self.rows, self.cols = index, grad, rows, cols
         self.width = cols[1] - cols[0]
         self.stages = []
-        size, land = rows, 0
-        for bit in bits:
-            halved = size % (2 * SUB) == 0
-            size = size // 2 if halved else size
-            self.stages.append((bit, size, halved, land))
-            land += size
-        self.land_rows = land
+        size, land, bits = rows, 0, []
+        for group in groups:
+            fits = size % (SUB << len(group)) == 0
+            for part in [group] if fits else [(bit,) for bit in group]:
+                halved = size % (SUB << len(part)) == 0
+                size = size >> len(part) if halved else size
+                self.stages.append((part, size, halved, land))
+                land += size * ((1 << len(part)) - 1)
+                bits.append(part)
+        self.bits, self.land_rows = bits, land
         self.steps = [("sum", i) for i in range(len(bits))]
         self.steps += [("get", i) for i in reversed(range(len(bits))) if self.stages[i][2]]
 
@@ -108,11 +111,15 @@
     xs = [("tm", 1 + k) for k in range(half)]
     ys = [("tm", 1 + half + k) for k in range(tm_bits - 1 - half)]
     zs = [("rows", k) for k in range(row_bits)]
-    axes = {"x": xs, "y": ys, "z": zs[:1]}
-
-    def order(first, second):
+
+    def order(name):
+        pair = name.isupper()
+        axes = {"x": [(b,) for b in xs], "y": [(b,) for b in ys]}
+        axes["z"] = [tuple(zs[:2])] if pair else [(b,) for b in zs[:1]]
+        first, second = name.lower()
         third = ({"x", "y", "z"} - {first, second}).pop()
-        return core + axes[first] + axes[second] + axes[third] + zs[1:]
+        rest = [(b,) for b in zs[2 if pair else 1 :]]
+        return [(core[0],)] + axes[first] + axes[second] + axes[third] + rest
 
     chunks = {}
     count = 0
@@ -122,10 +129,10 @@
             step = next(steps)
             for k in range(0, cols, step):
                 chunks[name, l, k] = Chunk(
-                    count, (name, l), rows, (k, k + step), order(*next(plan))
+                    count, (name, l), rows, (k, k + step), order(next(plan))
                 )
                 count += 1
-    chunks["s"] = Chunk(count, ("s", None), 2 * SUB, (0, width), order("y", "x"))
+    chunks["s"] = Chunk(count, ("s", None), 2 * SUB, (0, width), order("yx"))
     return chunks
 
 
@@ -150,9 +157,19 @@
     def coord(self, bit):
         return lax.rem(self.at[bit[0]] // (1 << bit[1]), 2)
 
-    def peer(self, bit):
-        own = self.at[bit[0]]
-        return {bit[0]: own + (1 - 2 * self.coord(bit)) * (1 << bit[1])}
+    def peer(self, bits):
+        ids = {}
+        for bit in bits:
+            own = ids.get(bit[0], self.at[bit[0]])
+            ids[bit[0]] = own + (1 - 2 * self.coord(bit)) * (1 << bit[1])
+        return ids
+
+    def share(self, bits, other=()):
+        part = 0
+        for bit in bits:
+            own = self.coord(bit)
+            part = 2 * part + (1 - own if bit in other else own)
+        return part
 
     def begin(self, chunk, level):
         key = (chunk.rows, tuple(chunk.bits[:level]))
@@ -160,9 +177,9 @@
             if level == 0:
                 self.starts[key] = 0
             else:
-                bit, size, halved, _ = chunk.stages[level - 1]
+                bits, size, halved, _ = chunk.stages[level - 1]
                 before = self.begin(chunk, level - 1)
-                self.starts[key] = before + self.coord(bit) * size if halved else before
+                self.starts[key] = before + self.share(bits) * size if halved else before
         return self.starts[key]
 
     def view(self, chunk, start, size, done=False):
@@ -172,14 +189,15 @@
         l = chunk.grad[1]
         return ref.at[rows, cols] if l is None else ref.at[l, rows, cols]
 
-    def link(self, bit):
+    def link(self, bits):
+        bit = bits[0]
         if bit[0] == "rows":
             return "z"
         return "c" if bit[1] == 0 else ("x" if bit[1] <= self.half_bits else "y")
 
     def cost(self, chunk, k):
         bit, size, _, _ = chunk.stages[chunk.steps[k][1]]
-        return size * chunk.width * 4 / self.RATE[self.link(bit)]
+        return size * chunk.width * 4 / self.RATE[self.link(bit)] * (3 if len(bit) > 1 else 1)
 
     def left(self, chunk, k):
         total = 0.0
@@ -224,42 +242,51 @@
         self.clock += 1
         self.used[chunk.index, k] = (put, get, self.clock)
         if self.refs is not None:
-            if kind == "sum":
-                before = self.begin(chunk, i)
-                if halved:
-                    before = before + (1 - self.coord(bit)) * size
-                src = self.view(chunk, before, size)
-                dst = self.lands[chunk.index].at[pl.ds(land, size)]
-            else:
-                src = dst = self.view(chunk, self.begin(chunk, i + 1), size, True)
-            copy = pltpu.make_async_remote_copy(
-                src,
-                dst,
-                self.refs[2].at[put],
-                self.refs[3].at[get],
-                device_id=self.peer(bit),
-                device_id_type=MESH,
-            )
-            copy.start()
-            self.copies[chunk.index, k] = copy
+            self.copies[chunk.index, k] = copies = []
+            for m in range(1, 1 << len(bit)):
+                other = [b for n, b in enumerate(bit) if m >> n & 1]
+                if kind == "sum":
+                    before = self.begin(chunk, i)
+                    if halved:
+                        before = before + self.share(bit, other) * size
+                    src = self.view(chunk, before, size)
+                    dst = self.lands[chunk.index].at[pl.ds(land + (m - 1) * size, size)]
+                else:
+                    src = dst = self.view(chunk, self.begin(chunk, i + 1), size, True)
+                copy = pltpu.make_async_remote_copy(
+                    src,
+                    dst,
+                    self.refs[2].at[put],
+                    self.refs[3].at[get],
+                    device_id=self.peer(other),
+                    device_id_type=MESH,
+                )
+                copy.start()
+                copies.append(copy)
         link = self.link(bit)
         cost = self.cost(chunk, k)
-        far = link == "z" and bit[1] > 0
+        far = link == "z" and bit[-1][1] > 0
         began = max(self.now, self.free[link], self.free["mid"] if far else 0.0)
         self.free[link] = done = began + cost
         if far:
-            self.free["mid"] = done = began + 2 * cost
+            self.free["mid"] = done = began + cost * (2 if len(bit) == 1 else 4 / 3)
         self.pending.append((done + self.DELAY[link], chunk.index, k, chunk))
-        self.now += 0.04
+        self.now += 0.04 * ((1 << len(bit)) - 1)
 
     def finish(self, item):
         _, _, k, chunk = item
         kind, i = chunk.steps[k]
         bit, size, _, land = chunk.stages[i]
         real = self.refs is not None
-        copy = self.copies.get((chunk.index, k))
-        if real:
-            copy.wait()
+        copies = self.copies.get((chunk.index, k))
+        many = (1 << len(bit)) - 1
+        if real and many == 1:
+            copies[0].wait()
+        elif real:
+            whole = self.lands[chunk.index].at[pl.ds(land, many * size)]
+            put, get, _ = self.used[chunk.index, k]
+            pltpu.make_async_copy(whole, whole, self.refs[3].at[get]).wait()
+            pltpu.make_async_copy(whole, whole, self.refs[2].at[put]).wait()
         put, get, launched = self.used[chunk.index, k]
         self.clock += 1
         self.puts[put] = True
@@ -275,19 +302,23 @@
         start = self.begin(chunk, i + 1) if real else 0
 
         def add(off, rows):
-            self.now += rows * chunk.width * 4 / 3e6
+            self.now += rows * chunk.width * 4 / 3e6 * (many + 1) / 2
             if not real:
                 return
             ref = self.view(chunk, start + off, rows)
-            at = land + off
-            at = pl.multiple_of(at, SUB) if not isinstance(at, int) else at
+            total = ref[...]
+            for m in range(many):
+                at = land + m * size + off
+                at = pl.multiple_of(at, SUB) if not isinstance(at, int) else at
+                total = total + self.lands[chunk.index][pl.ds(at, rows), :]
             last = i + 1 == len(chunk.bits)
             into = self.view(chunk, start + off, rows, True) if last else ref
-            into[...] = ref[...] + self.lands[chunk.index][pl.ds(at, rows), :]
-
-        if i + 1 < len(chunk.bits) and chunk.stages[i + 1][2]:
+            into[...] = total
+
+        follows = chunk.stages[i + 1] if i + 1 < len(chunk.bits) else None
+        if follows is not None and follows[2] and len(follows[0]) == 1:
             half = size // 2
-            mine = self.coord(chunk.stages[i + 1][0]) if real else 0
+            mine = self.share(follows[0]) if real else 0
             add((1 - mine) * half, half)
             self.push(chunk, k + 1)
             self.pump()
@@ -351,7 +382,11 @@
     P2 = 2 * states
 
     barrier = pltpu.get_barrier_semaphore()
-    others = [lax.rem(at + k, n_tm) for k in range(1, n_tm)]
+    tm_bits = int(math.log2(n_tm))
+    others = []
+    for m in reversed(range(1, n_tm)):
+        flips = [(1 - 2 * lax.rem(at // (1 << b), 2)) * (1 << b) for b in range(tm_bits) if m >> b & 1]
+        others.append(at + sum(flips))
     for other in others:
         pl.semaphore_signal(barrier, inc=1, device_id={"tm": other}, device_id_type=MESH)
     row_at = lax.axis_index("rows")
@@ -361,10 +396,10 @@
     half_bits = (int(math.log2(n_tm)) - 1) // 2
     mover = Mover(chunks, mover_refs, lands, {"tm": at, "rows": row_at}, half_bits)
     row_bits = int(math.log2(n_rows))
-    for k in range(row_bits):
-        pl.semaphore_signal(
-            barrier, inc=1, device_id=mover.peer(("rows", k)), device_id_type=MESH
-        )
+    zs = [("rows", k) for k in range(row_bits)]
+    greeted = [[z] for z in zs] + ([zs[:2]] if row_bits > 1 else [])
+    for bits in greeted:
+        pl.semaphore_signal(barrier, inc=1, device_id=mover.peer(bits), device_id_type=MESH)
 
     def load(k, src, dst):
         copy = pltpu.make_async_copy(src, dst, R.in_sem.at[k])
@@ -565,7 +600,7 @@
         R.msg[e, r, :, states:P2] = seen[1][last]
         R.msg[e, r, :, P2 : P2 + 128] = total_mask[r]
         if first_wait[0]:
-            pl.semaphore_wait(barrier, n_tm - 1 + row_bits)
+            pl.semaphore_wait(barrier, n_tm - 1 + len(greeted))
             first_wait[0] = False
         for other in others:
             copy = pltpu.make_async_remote_copy(

time: 93.2 us -> 91 us (0.976)
  Pallas kernels: 92.2 us -> 90 us
    pallas_call x1, Pallas kernels: 88.5 us -> 86.3 us  [on_device(): pl.pallas_call(functools.partial(kernel, cfg), out_shape=[pltpu.VMEM(o.sh...]
where the time goes in v3:
time: 91 us; the launch traced here: 90.9 us
  Pallas kernels  90 us (99%)
    pallas_call x1, Pallas kernels, on_device(): pl.pallas_call(functools.partial(kernel, cfg), out_shape=[pltpu.VMEM(o.sh...  86.3 us
    pallas_call x1, Pallas kernels, on_device(): pl.pallas_call(functools.partial(finish_kernel, states), out_shape=final_...  3.74 us

profile of v3, /device:TPU:0, one launch (start us, length us, event | category | flops | bytes accessed | tf_op | source)
XLA Modules:
  0.0 90.9 jit_solution(16076675881062951130)
XLA Ops:
  0.7 86.3 %shard_map.237 = (bf16[2,256,512]{2,1,0:T(8,128)(2,1)S(1)}, bf16[2,256,512]{2,1,0:T(8,128)(2,1)S(1)}, f32[16,512]{1,0:T(8,128)S(1)}, f32[2,512,768]{2,1,0:T(8,12...) custom-call(bf16[2,256,512]{2,1,0:T(8,128)(2,1)} %refs_0_.1, s32[2,256]{1,0:T(2,128)} %refs_1_.1, ...), custom_call_target="tpu_custom_call" | custom-call | tf_op jit(solution)/shard_map/pallas_call | solution.py:902
  87.0 3.7 %shard_map.238 = (bf16[2,256,512]{2,1,0:T(8,128)(2,1)}, bf16[2,256,512]{2,1,0:T(8,128)(2,1)}, f32[2,512]{1,0:T(2,128)}, f32[2,384]{1,0:T(2,128)}, f32[2,384]{1,0...) custom-call(bf16[2,256,512]{2,1,0:T(8,128)(2,1)S(1)} %get-tuple-elem, ...), custom_call_target="tpu_custom_call" | custom-call | tf_op jit(solution)/shard_map/pallas_call | solution.py:916

commit v4 on v3

--- a/solution.py
+++ b/solution.py
@@ -16,10 +16,10 @@
 UNROLL = 16
 PUTS, GETS = 24, 15
 TILE = 256
-STEPS = [256, 128, 128, 256, 128, 128]
+STEPS = [128, 128, 256, 256, 128, 128]
 ORDERS = [
-    "zy", "XY", "yx", "xy", "YX", "ZX", "ZY", "yx", "yx", "yx", "YX", "XY", "XY", "yx", "xz",
-    "xy", "YX", "zx", "YX", "YX", "yx", "xy", "xy", "xz",
+    "YX", "XY", "YX", "ZX", "yx", "XY", "zy", "ZY", "YX", "xy", "zx", "yx", "xy", "xy", "XY",
+    "YX", "yz", "YX", "xy", "XY", "xy", "xy", "yz",
 ]
 
 
@@ -456,13 +456,16 @@
     def inside(forward, by):
         return seg_id >= by if forward else seg_id < SUB - by
 
-    window, excl, total_mask = {}, {}, {}
+    window, excl, total_mask, whole = {}, {}, {}, {}
     for r in range(rows_dev):
         places = [R.keep[r * group + j * SUB : r * group + (j + 1) * SUB] for j in range(per_seg)]
         while len(places) > 1:
             places = [a * b for a, b in zip(places[::2], places[1::2])]
-        for forward in (True, False):
-            run, seen = places[0], places[0]
+        whole[r] = places[0]
+
+    def masks(forward):
+        for r in range(rows_dev):
+            run, seen = whole[r], whole[r]
             for by in (1, 2, 4):
                 ok = inside(forward, by)
                 window[r, forward, by] = jnp.where(ok, run, 0.0)
@@ -472,8 +475,7 @@
             if forward:
                 total_mask[r] = seen[SUB - 1 : SUB]
 
-    L = []
-    for l in range(2):
+    def constants(l):
         lam = [n[l : l + 1, :] for n in (R.lam_re, R.lam_im, R.steps)]
         a_re, a_im, q_re, q_im = discretize(*lam)
         power = (a_re, a_im)
@@ -491,7 +493,7 @@
                     jnp.where((index & by) != 0, m, o) for m, o in zip(more, at_seg)
                 )
             powers[forward, 0] = at_seg
-        L.append(dict(lam=lam, a=(a_re, a_im), q=(q_re, q_im), powers=powers, l=l))
+        return dict(lam=lam, a=(a_re, a_im), q=(q_re, q_im), powers=powers, l=l)
 
     def input_matrix(layer, m_ref):
         q_re, q_im = layer["q"]
@@ -727,7 +729,8 @@
             row = 6 + 2 * k + l
             R.small_g[row : row + 1, 0:states] = grad
 
-    one, two = L
+    one = constants(0)
+    masks(True)
     for cp in cp_b:
         cp.wait()
     input_matrix(one, R.m1)
@@ -741,6 +744,8 @@
             norm_front(h, one, R.z1, R.r1, R.u1, R.m1, sl)
         ends, _ = scan_pass(r, one, True, zero_state, None)
         sent[0, r] = send_carry(0, r, one, True, ends)
+    two = constants(1)
+    masks(False)
     for cp in cp_c + cp_w + cp_t:
         cp.wait()
     input_matrix(two, R.m2)
@@ -778,9 +783,13 @@
     da2, da1 = Adjoint(R.x2, R.dv2).zero(), Adjoint(R.x1, R.dv1).zero()
     for r in rows:
         carry = take_carry(2, r, two, True, sent[2, r])
-        mover.run(0.3)
         _, da = scan_pass(r, two, True, carry, Adjoint(R.x2, R.dv2))
         da2 = (da2[0] + da[0], da2[1] + da[1])
+        mover.run(0.3)
+    R.small_g[...] = jnp.zeros((2 * SUB, width), F32)
+    matrix_grads(two, R.u2, R.dv2, da2)
+    mover.run(0.8)
+    for r in rows:
         mover.run(0.3)
         for sl, _ in tiles[r]:
             d_mid = back_norm(two, R.d_mid[sl, :], R.dv2, R.m2, R.dy2, R.z2, R.r2, sums2, sl)
@@ -793,9 +802,6 @@
         ends, _ = scan_pass(r, one, False, zero_state, None)
         mover.run(0.3)
         sent[3, r] = send_carry(3, r, one, False, ends)
-    R.small_g[...] = jnp.zeros((2 * SUB, width), F32)
-    matrix_grads(two, R.u2, R.dv2, da2)
-    mover.run(0.8)
     product_grads(one, R.gl1, R.ds1, R.s1, R.dy1)
 
     for r in rows:

time: 91 us -> 88.9 us (0.977)
  Pallas kernels: 90 us -> 87.9 us
    pallas_call x1, Pallas kernels: 86.3 us -> 84.1 us  [on_device(): pl.pallas_call(functools.partial(kernel, cfg), out_shape=[pltpu.VMEM(o.sh...]
where the time goes in v4:
time: 88.9 us; the launch traced here: 88.7 us
  Pallas kernels  87.9 us (99%)
    pallas_call x1, Pallas kernels, on_device(): pl.pallas_call(functools.partial(kernel, cfg), out_shape=[pltpu.VMEM(o.sh...  84.1 us
    pallas_call x1, Pallas kernels, on_device(): pl.pallas_call(functools.partial(finish_kernel, states), out_shape=final_...  3.74 us

profile of v4, /device:TPU:0, one launch (start us, length us, event | category | flops | bytes accessed | tf_op | source)
XLA Modules:
  0.0 88.7 jit_solution(14387569970611599059)
XLA Ops:
  0.7 84.1 %shard_map.237 = (bf16[2,256,512]{2,1,0:T(8,128)(2,1)S(1)}, bf16[2,256,512]{2,1,0:T(8,128)(2,1)S(1)}, f32[16,512]{1,0:T(8,128)S(1)}, f32[2,512,768]{2,1,0:T(8,12...) custom-call(bf16[2,256,512]{2,1,0:T(8,128)(2,1)} %refs_0_.1, s32[2,256]{1,0:T(2,128)} %refs_1_.1, ...), custom_call_target="tpu_custom_call" | custom-call | tf_op jit(solution)/shard_map/pallas_call | solution.py:908
  84.8 3.7 %shard_map.238 = (bf16[2,256,512]{2,1,0:T(8,128)(2,1)}, bf16[2,256,512]{2,1,0:T(8,128)(2,1)}, f32[2,512]{1,0:T(2,128)}, f32[2,384]{1,0:T(2,128)}, f32[2,384]{1,0...) custom-call(bf16[2,256,512]{2,1,0:T(8,128)(2,1)S(1)} %get-tuple-elem, ...), custom_call_target="tpu_custom_call" | custom-call | tf_op jit(solution)/shard_map/pallas_call | solution.py:922

commit v5 on v4

--- a/solution.py
+++ b/solution.py
@@ -387,8 +387,6 @@
     for m in reversed(range(1, n_tm)):
         flips = [(1 - 2 * lax.rem(at // (1 << b), 2)) * (1 << b) for b in range(tm_bits) if m >> b & 1]
         others.append(at + sum(flips))
-    for other in others:
-        pl.semaphore_signal(barrier, inc=1, device_id={"tm": other}, device_id_type=MESH)
     row_at = lax.axis_index("rows")
     grads = {"b": R.b_g, "c": R.c_g, "w": R.w_g, "s": R.small_g}
     sums = {"b": R.b_o, "c": R.c_o, "w": R.w_o, "s": R.small_o}
@@ -398,8 +396,6 @@
     row_bits = int(math.log2(n_rows))
     zs = [("rows", k) for k in range(row_bits)]
     greeted = [[z] for z in zs] + ([zs[:2]] if row_bits > 1 else [])
-    for bits in greeted:
-        pl.semaphore_signal(barrier, inc=1, device_id=mover.peer(bits), device_id_type=MESH)
 
     def load(k, src, dst):
         copy = pltpu.make_async_copy(src, dst, R.in_sem.at[k])
@@ -415,6 +411,10 @@
     cp_small = [load(k0 + k, src, dst) for k, (src, dst) in enumerate(pairs)]
     k0 = rows_dev
     cp_b = [load(k0, R.b_re.at[0], R.wb_re.at[0]), load(k0 + 1, R.b_im.at[0], R.wb_im.at[0])]
+    for other in others:
+        pl.semaphore_signal(barrier, inc=1, device_id={"tm": other}, device_id_type=MESH)
+    for bits in greeted:
+        pl.semaphore_signal(barrier, inc=1, device_id=mover.peer(bits), device_id_type=MESH)
     cp_c = [
         load(k0 + 2, R.c_re, R.wc.at[:, pl.ds(0, states)]),
         load(k0 + 3, R.c_im, R.wc.at[:, pl.ds(states, states)]),

time: 88.9 us -> 88.8 us (level)
  no operation moved by 1% of the time
where the time goes in v5:
time: 88.8 us; the launch traced here: 88.7 us
  Pallas kernels  87.9 us (99%)
    pallas_call x1, Pallas kernels, on_device(): pl.pallas_call(functools.partial(kernel, cfg), out_shape=[pltpu.VMEM(o.sh...  84.1 us
    pallas_call x1, Pallas kernels, on_device(): pl.pallas_call(functools.partial(finish_kernel, states), out_shape=final_...  3.74 us

profile of v5, /device:TPU:0, one launch (start us, length us, event | category | flops | bytes accessed | tf_op | source)
XLA Modules:
  0.0 88.7 jit_solution(14401817537260802298)
XLA Ops:
  0.7 84.1 %shard_map.237 = (bf16[2,256,512]{2,1,0:T(8,128)(2,1)S(1)}, bf16[2,256,512]{2,1,0:T(8,128)(2,1)S(1)}, f32[16,512]{1,0:T(8,128)S(1)}, f32[2,512,768]{2,1,0:T(8,12...) custom-call(bf16[2,256,512]{2,1,0:T(8,128)(2,1)} %refs_0_.1, s32[2,256]{1,0:T(2,128)} %refs_1_.1, ...), custom_call_target="tpu_custom_call" | custom-call | tf_op jit(solution)/shard_map/pallas_call | solution.py:908
  84.8 3.7 %shard_map.238 = (bf16[2,256,512]{2,1,0:T(8,128)(2,1)}, bf16[2,256,512]{2,1,0:T(8,128)(2,1)}, f32[2,512]{1,0:T(2,128)}, f32[2,384]{1,0:T(2,128)}, f32[2,384]{1,0...) custom-call(bf16[2,256,512]{2,1,0:T(8,128)(2,1)S(1)} %get-tuple-elem, ...), custom_call_target="tpu_custom_call" | custom-call | tf_op jit(solution)/shard_map/pallas_call | solution.py:922
